TPU v7x, 128 devices: a whole 4x4x4 slice. The times are simulated.
128 devices in a mesh: band: 8 (over z, core), sector: 16 (over x, y).
Axes of the slice: x: 4, y: 4, z: 4, core: 2. Of those that a mesh axis runs over, the one named last changes fastest.
Arguments:
- base_state: float32 [128, 256, 1536], P('band', 'sector'), may hold values from -6 to 6
- direction: float32 [128, 256, 1536], P('band', 'sector'), may hold values from -24 to 24
- residual: float32 [128, 256, 1536], P('band', 'sector'), may hold values from -24 to 24
- mix_coef: float32 [9, 1536], replicated, may hold values from -2.5 to 2.5
- w_in: bfloat16 [1536, 3072], replicated, may hold values from -0.15625 to 0.15625
- w_out: bfloat16 [3072, 1536], replicated, may hold values from -0.109375 to 0.109375
- obs_patch: int32 [128, 128, 4], P(('band', 'sector')), may hold values from 0 to 255
- obs_count: int32 [128, 128], P(('band', 'sector')), may hold values from 0 to 4, as said below
- obs_pos: int32 [128, 128, 4, 4], P(('band', 'sector')), may hold values from 0 to 1535
- obs_wgt: float32 [128, 128, 4, 4], P(('band', 'sector')), may hold values from 0.2 to 1
- obs_rinv: float32 [128, 128, 4], P(('band', 'sector')), may hold values from 1 to 1500
Outputs:
- next_residual: float32 [128, 256, 1536], P('band', 'sector')
Inputs may be any that keep to these rules, and one draw needn't show every extreme that they name: `obs_count`: live station slots of one owner for one source block are that pair's first slots; in every draw some source block has all 4 slots live from every owner.
All inputs are finite; a program needn't handle non-finite values.
Results may differ from a plain program's by a relative error of at most 0.006.
Values may be sent and summed in bfloat16 or wider, within the bound.
A program may use at most 128 MiB of HBM per device.

v0:
```python
import math

import jax
import jax.numpy as jnp
from jax import lax
from jax.sharding import PartitionSpec as P


def padded_2(block, sides, width, periodic):
    for axis, dim in sides:
        count = lax.axis_size(axis)
        forward = [(i, i + 1) for i in range(count - 1)]
        if periodic:
            forward.append((count - 1, 0))
        backward = [(target, source) for source, target in forward]
        low = lax.ppermute(
            lax.slice_in_dim(block, block.shape[dim] - width, None, axis=dim), axis, forward
        )
        high = lax.ppermute(lax.slice_in_dim(block, 0, width, axis=dim), axis, backward)
        block = jnp.concatenate([low, block, high], axis=dim)
    return block


def gelu_slope(preact):
    normal_cdf = 0.5 * (1.0 + jax.scipy.special.erf(preact * (1.0 / math.sqrt(2.0))))
    normal_pdf = jnp.exp(-0.5 * preact * preact) * (1.0 / math.sqrt(2.0 * math.pi))
    return normal_cdf + preact * normal_pdf


def extend(stacked):
    lon_wide = padded_2(stacked, (("sector", 2),), 1, True)
    return padded_2(lon_wide, (("band", 1),), 1, False)


def stencil_apply(padded, mix_coef, lat_n, lon_n):
    summed = jnp.zeros((lat_n, lon_n, mix_coef.shape[1]), jnp.float32)
    for row_off in range(3):
        for col_off in range(3):
            summed = (
                summed
                + mix_coef[3 * row_off + col_off]
                * padded[row_off : row_off + lat_n, col_off : col_off + lon_n]
            )
    return summed


def stencil_adjoint(padded, mix_coef, lat_n, lon_n):
    summed = jnp.zeros((lat_n, lon_n, mix_coef.shape[1]), jnp.float32)
    for row_off in range(3):
        for col_off in range(3):
            summed = (
                summed
                + mix_coef[3 * row_off + col_off]
                * padded[2 - row_off : 2 - row_off + lat_n, 2 - col_off : 2 - col_off + lon_n]
            )
    return summed


def weigh(sampled, counts, weights_tap, rinv):
    slot_n = weights_tap.shape[-2]
    active = (jnp.arange(slot_n, dtype=jnp.int32) < counts[..., None]).astype(jnp.float32)
    misfit = jnp.sum(weights_tap * sampled, axis=-1)
    return (active * rinv * misfit)[..., None] * weights_tap


def shards(
    base_state,
    direction,
    residual,
    mix_coef,
    w_in,
    w_out,
    obs_patch,
    obs_count,
    obs_pos,
    obs_wgt,
    obs_rinv,
):
    lat_n, lon_n, features = base_state.shape
    tok_n = lat_n * lon_n
    norm_sq = lax.psum(jnp.sum(residual * residual), ("band", "sector"))
    stacked = extend(jnp.stack([base_state, direction]))
    mix_base = (
        stencil_apply(stacked[0], mix_coef, lat_n, lon_n)
        .astype(jnp.bfloat16)
        .reshape(tok_n, features)
    )
    preact = jnp.dot(mix_base, w_in, preferred_element_type=jnp.float32)
    slopes = gelu_slope(preact)
    tangent_mix = (
        stencil_apply(stacked[1], mix_coef, lat_n, lon_n)
        .astype(jnp.bfloat16)
        .reshape(tok_n, features)
    )
    tangent_hidden = (
        slopes * jnp.dot(tangent_mix, w_in, preferred_element_type=jnp.float32)
    ).astype(jnp.bfloat16)
    tangent = (
        direction.reshape(tok_n, features)
        + jnp.dot(tangent_hidden, w_out, preferred_element_type=jnp.float32)
    ).astype(jnp.bfloat16)
    wanted = lax.all_to_all(obs_patch, ("band", "sector"), split_axis=1, concat_axis=0, tiled=True)
    fetched = tangent[wanted]
    arrived = lax.all_to_all(fetched, ("band", "sector"), split_axis=0, concat_axis=1, tiled=True)
    sampled = jnp.take_along_axis(arrived, obs_pos, axis=3).astype(jnp.float32)
    deposit = weigh(sampled, obs_count, obs_wgt, obs_rinv)
    channel_ids = jnp.arange(features, dtype=jnp.int32)
    row_grad = jnp.zeros(arrived.shape, jnp.float32)
    for tap_idx in range(deposit.shape[-1]):
        picked = (obs_pos[..., tap_idx : tap_idx + 1] == channel_ids).astype(jnp.float32)
        row_grad = row_grad + deposit[..., tap_idx : tap_idx + 1] * picked
    returned = lax.all_to_all(row_grad, ("band", "sector"), split_axis=1, concat_axis=0, tiled=True)
    obs_grad = (
        jnp.zeros((tok_n, features), jnp.float32)
        .at[wanted.reshape(-1)]
        .add(returned.reshape(-1, features))
    )
    grad_hidden = jnp.dot(
        obs_grad.astype(jnp.bfloat16), w_out.T, preferred_element_type=jnp.float32
    )
    grad_act = (slopes * grad_hidden).astype(jnp.bfloat16)
    grad_mix = jnp.dot(grad_act, w_in.T, preferred_element_type=jnp.float32).reshape(
        1, lat_n, lon_n, features
    )
    grad_padded = extend(grad_mix)[0]
    hess_vec = (
        direction
        + obs_grad.reshape(lat_n, lon_n, features)
        + stencil_adjoint(grad_padded, mix_coef, lat_n, lon_n)
    )
    curvature = lax.psum(jnp.sum(direction * hess_vec), ("band", "sector"))
    return residual - norm_sq / curvature * hess_vec


def solution(mesh):
    return jax.shard_map(
        shards,
        mesh=mesh,
        in_specs=(
            P("band", "sector", None),
            P("band", "sector", None),
            P("band", "sector", None),
            P(),
            P(),
            P(),
            P(("band", "sector"), None, None),
            P(("band", "sector"), None),
            P(("band", "sector"), None, None, None),
            P(("band", "sector"), None, None, None),
            P(("band", "sector"), None, None),
        ),
        out_specs=P("band", "sector", None),
        check_vma=False,
    )
```

profile of v0, /device:TPU:1, one launch (start us, length us, event | category | flops | bytes accessed | tf_op | source)
XLA Modules:
  0.0 279.7 jit_solution(2249113664078254912)
XLA Ops:
  0.0 3.0 %pad_maximum_fusion.6 = (f32[2,16,1,1536]{3,2,1,0:T(1,128)}, f32[2,16,1,1536]{3,2,1,0:T(1,128)}) fusion(f32[1,16,16,1536]{3,2,1,0:T(8,128)} %bitcast.51, f32[1,16,16,1536]{3,2,1,0:T(8,128)} %bitcast.55), kind=kLoop, calls=%fused_computation.89 | loop fusion | flops 98304 | bytes 3538944 | tf_op jit(solution)/shard_map/slice | solution.py:17
  5.2 3.6 %collective-permute-start.1 = (f32[2,16,1,1536]{3,2,1,0:T(1,128)}, f32[2,16,1,1536]{3,2,1,0:T(1,128)S(1)}, u32[]{:S(2)}, u32[]{:S(2)}) collective-permute-start(f32[2,16,1,1536]{3,2,1,0:T(1,128)} %get-tuple-element.23), channel_id=1, source_target_pairs={{1,0},{2,1},{3,2},{4,3},{5,4},{6,5},{7,6},{8,7},{9,8},{10,9},{11,1... | collective-permute-start | bytes 589832 | tf_op jit(solution)/shard_map/ppermute | solution.py:19
  9.6 8.2 %all-to-all-start = ((s32[1,128,4]{2,0,1:T(1,128)}), s32[1,128,4]{2,0,1:T(1,128)}, u32[]{:S(2)}, u32[]{:S(2)}) async-start(s32[1,128,4]{2,0,1:T(1,128)} %copy.52), calls=%async_computation | async-start | bytes 131072 | tf_op jit(solution)/shard_map/all_to_all | solution.py:102
  20.8 3.7 %collective-permute-start.2 = (f32[2,1,18,1536]{3,2,1,0:T(8,128)}, f32[2,1,18,1536]{3,2,1,0:T(8,128)}, u32[]{:S(2)}, u32[]{:S(2)}) collective-permute-start(f32[2,1,18,1536]{3,2,1,0:T(8,128)} %get-tuple-element.20), channel_id=1, source_target_pairs={{0,16},{16,32},{32,48},{48,64},{64,80},{80,96},{96,112},{1,17},{17... | collective-permute-start | bytes 663560 | tf_op jit(solution)/shard_map/ppermute | solution.py:16
  29.6 3.1 %collective-permute-done.3 = f32[2,1,18,1536]{3,2,1,0:T(8,128)} collective-permute-done((f32[2,1,18,1536]{3,2,1,0:T(8,128)}, f32[2,1,18,1536]{3,2,1,0:T(8,128)}, u32[]{:S(2)}, u32[]{:S(2)}) %collective-permute-start.3) | collective-permute-done | bytes 221216 | tf_op jit(solution)/shard_map/ppermute | solution.py:19
  39.4 4.3 %fusion.55 = f32[256,3072]{1,0:T(8,128)} fusion(bf16[256,1536]{1,0:T(8,128)(2,1)S(1)} %bitcast.63, bf16[1536,3072]{1,0:T(8,128)(2,1)S(1)} %bitcast.76), kind=kOutput, calls=%fused_computation.124 | convolution fusion | flops 2415919104 | bytes 13369344 | tf_op jit(solution)/shard_map/dot_general | solution.py:88
  43.7 10.3 %fusion.6 = bf16[256,1536]{1,0:T(8,128)(2,1)S(1)} fusion(f32[256,1536]{1,0:T(8,128)S(1)} %bitcast.54, bf16[3072,1536]{1,0:T(8,128)(2,1)} %param.16, bf16[256,1536]{1,0:T(8,128)(2,1)S(1)} %bitcast.64, bf16[1536,3072]{1,0:T(8,128)(2,1)} %param.15, f32[256,3072]{1,0:T(8,128)} %fusion.55), kind=kOutput, calls=%fused_computation.22 | convolution fusion | flops 4840488960 | bytes 25165824 | tf_op jit(solution)/shard_map/dot_general | solution.py:100
  53.9 2.9 %gather_fusion = bf16[512,1536]{1,0:T(8,128)(2,1)} fusion(bf16[256,1536]{1,0:T(8,128)(2,1)S(1)} %fusion.6, s32[1024]{0:T(1024)S(1)} %pad_clamp_fusion), kind=kCustom, calls=%fused_computation | custom fusion | bytes 3147776 | tf_op jit(solution)/shard_map/gather | solution.py:103
  56.9 3.9 %reshape.254 = bf16[128,1,4,1536]{3,2,0,1:T(4,128)(2,1)} reshape(bf16[512,1536]{1,0:T(8,128)(2,1)} %gather_fusion) | data formatting | bytes 3145728 | tf_op jit(solution)/shard_map/gather | solution.py:103
  60.7 9.2 %all-to-all-start.1 = ((bf16[128,1,4,1536]{3,2,1,0:T(4,128)(2,1)}), bf16[128,1,4,1536]{3,2,1,0:T(4,128)(2,1)S(1)}, u32[]{:S(2)}, u32[]{:S(2)}) async-start(bf16[128,1,4,1536]{3,2,1,0:T(4,128)(2,1)} %bitcast.62), calls=%async_computation.1 | async-start | bytes 3145728 | tf_op jit(solution)/shard_map/all_to_all | solution.py:104
  70.9 23.2 %all-to-all-done.1 = bf16[128,1,4,1536]{3,2,1,0:T(4,128)(2,1)S(1)} async-done(((bf16[128,1,4,1536]{3,2,1,0:T(4,128)(2,1)}), bf16[128,1,4,1536]{3,2,1,0:T(4,128)(2,1)S(1)}, u32[]{:S(2)}, u32[]{:S(2)}) %all-to-all-start.1) | async-done | bytes 1572896 | tf_op jit(solution)/shard_map/all_to_all | solution.py:104
  94.1 20.4 %gather_fusion.1 = bf16[2048]{0:T(1024)(128)(2,1)S(1)} fusion(bf16[128,4,1536]{2,1,0:T(4,128)(2,1)S(1)} %bitcast.50, s32[2048]{0:T(1024)S(1)} %reshape.263), kind=kCustom, calls=%fused_computation.1 | custom fusion | bytes 32768 | tf_op jit(solution)/shard_map/jit(take_along_axis)/gather | solution.py:105
  115.4 4.4 %select_add_fusion = f32[1,128,4,1536]{3,2,0,1:T(4,128)} fusion(f32[128,4]{1,0:T(8,128)S(1)} %copy.63, s32[128,4]{1,0:T(8,128)S(1)} %copy.62, f32[128,4]{1,0:T(8,128)S(1)} %copy.61, s32[128,4]{1,0:T(8,128)S(1)} %copy.60, f32[128,4]{1,0:T(8,128)S(1)} %copy.59, s32[128,4]{1,0:T(8,128)S(1)} %copy.58, f32[128,4]{1,0:T(8,128)S(1)} %copy.57, s32[128,4]{1,0:T(8,128)S(1)} %copy.53), kind=kLoop, calls=%fused_computation.13 | loop fusion | flops 8650752 | bytes 3162112 | tf_op jit(solution)/shard_map/add | solution.py:111
  119.8 5.8 %all-to-all-start.2 = ((f32[1,128,4,1536]{3,2,0,1:T(4,128)}), f32[1,128,4,1536]{3,2,0,1:T(4,128)}, u32[]{:S(2)}, u32[]{:S(2)}) async-start(f32[1,128,4,1536]{3,2,0,1:T(4,128)} %select_add_fusion), calls=%async_computation.2 | async-start | bytes 6291456 | tf_op jit(solution)/shard_map/all_to_all | solution.py:112
  127.9 38.6 %all-to-all-done.2 = f32[1,128,4,1536]{3,2,0,1:T(4,128)} async-done(((f32[1,128,4,1536]{3,2,0,1:T(4,128)}), f32[1,128,4,1536]{3,2,0,1:T(4,128)}, u32[]{:S(2)}, u32[]{:S(2)}) %all-to-all-start.2) | async-done | bytes 3145760 | tf_op jit(solution)/shard_map/all_to_all | solution.py:112
  166.5 4.9 %reshape.273 = f32[512,1536]{1,0:T(8,128)} reshape(f32[1,128,4,1536]{3,2,0,1:T(4,128)} %all-to-all-done.2) | data formatting | bytes 6291456 | tf_op jit(solution)/shard_map/reshape | solution.py:116
  171.5 8.0 %scatter_custom_fusion = f32[256,1536]{1,0:T(8,128)} fusion(s32[512]{0:T(512)S(1)} %bitcast.73, f32[512,1536]{1,0:T(8,128)} %reshape.273, f32[]{:T(128)} %constant.11.clone.1), kind=kCustom, calls=%fused_computation.81 | custom fusion | flops 786432 | bytes 1573376 | tf_op jit(solution)/shard_map/scatter-add | solution.py:116
  179.4 10.6 %fusion.38 = f32[256,1536]{1,0:T(8,128)S(1)} fusion(bf16[1536,3072]{1,0:T(8,128)(2,1)} %param.15, bf16[3072,1536]{1,0:T(8,128)(2,1)} %param.16, f32[256,1536]{1,0:T(8,128)} %scatter_custom_fusion, f32[256,3072]{1,0:T(8,128)} %fusion.55), kind=kOutput, calls=%fused_computation.83 | convolution fusion | flops 4840095744 | bytes 25165824 | tf_op jit(solution)/shard_map/dot_general | solution.py:122
  190.7 4.4 %collective-permute-start.5 = (f32[1,16,1,1536]{3,2,1,0:T(1,128)S(1)}, f32[1,16,1,1536]{3,2,1,0:T(1,128)S(1)}, u32[]{:S(2)}, u32[]{:S(2)}) collective-permute-start(f32[1,16,1,1536]{3,2,1,0:T(1,128)S(1)} %get-tuple-element.27), channel_id=1, source_target_pairs={{1,0},{2,1},{3,2},{4,3},{5,4},{6,5},{7,6},{8,7},{9,8},{10,9},{11,1... | collective-permute-start | bytes 294920 | tf_op jit(solution)/shard_map/ppermute | solution.py:19
  197.5 3.6 %collective-permute-start.6 = (f32[1,1,18,1536]{3,2,1,0:T(8,128)S(1)}, f32[1,1,18,1536]{3,2,1,0:T(8,128)S(1)}, u32[]{:S(2)}, u32[]{:S(2)}) collective-permute-start(f32[1,1,18,1536]{3,2,1,0:T(8,128)S(1)} %get-tuple-element.24), channel_id=1, source_target_pairs={{0,16},{16,32},{32,48},{48,64},{64,80},{80,96},{96,112},{1,17},{17... | collective-permute-start | bytes 331784 | tf_op jit(solution)/shard_map/ppermute | solution.py:16
  204.1 3.5 %collective-permute-done.7 = f32[1,1,18,1536]{3,2,1,0:T(8,128)S(1)} collective-permute-done((f32[1,1,18,1536]{3,2,1,0:T(8,128)S(1)}, f32[1,1,18,1536]{3,2,1,0:T(8,128)S(1)}, u32[]{:S(2)}, u32[]{:S(2)}) %collective-permute-start.7) | collective-permute-done | bytes 110624 | tf_op jit(solution)/shard_map/ppermute | solution.py:19
  208.0 2.6 multiply_reduce_fusion
  210.6 65.0 %all-reduce = (f32[]{:T(128)}, f32[]{:T(128)}) all-reduce(f32[]{:T(128)} %multiply_reduce_fusion.1, f32[]{:T(128)} %get-tuple-element.16), channel_id=1, replica_groups=mesh['band'=8,'sector'=16] {'band','sector'}, use_global_device_ids=true, to_apply=%region_1.0 | all-reduce | flops 2 | bytes 16 | tf_op jit(solution)/shard_map/psum | solution.py:81
  276.9 2.8 multiply_subtract_fusion
  (88 shorter events, 28.1 us)
Async XLA Ops:
  0.0 8.8 %copy-start.14 = (s32[1,128,4]{1,2,0:T(4,128)S(1)}, s32[1,128,4]{1,2,0:T(4,128)}, u32[]{:S(2)}) copy-start(s32[1,128,4]{1,2,0:T(4,128)} %param.17) | copy-start | bytes 6148
  0.0 19.9 %copy-start = (f32[16,16,1536]{2,1,0:T(8,128)S(1)}, f32[16,16,1536]{2,1,0:T(8,128)}, u32[]{:S(2)}) copy-start(f32[16,16,1536]{2,1,0:T(8,128)} %param.12) | copy-start | bytes 4718596
  0.0 19.9 %copy-start.1 = (f32[16,16,1536]{2,1,0:T(8,128)S(1)}, f32[16,16,1536]{2,1,0:T(8,128)}, u32[]{:S(2)}) copy-start(f32[16,16,1536]{2,1,0:T(8,128)} %param.11) | copy-start | bytes 4718596
  3.1 16.8 %collective-permute-start = (f32[2,16,1,1536]{3,2,1,0:T(1,128)}, f32[2,16,1,1536]{3,2,1,0:T(1,128)S(1)}, u32[]{:S(2)}, u32[]{:S(2)}) collective-permute-start(f32[2,16,1,1536]{3,2,1,0:T(1,128)} %get-tuple-element.22), channel_id=1, source_target_pairs={{0,1},{1,2},{2,3},{3,4},{4,5},{5,6},{6,7},{7,8},{8,9},{9,10},{10,1... | collective-permute-start | bytes 589832 | tf_op jit(solution)/shard_map/ppermute | solution.py:16
  5.2 14.7 %collective-permute-start.1 = (f32[2,16,1,1536]{3,2,1,0:T(1,128)}, f32[2,16,1,1536]{3,2,1,0:T(1,128)S(1)}, u32[]{:S(2)}, u32[]{:S(2)}) collective-permute-start(f32[2,16,1,1536]{3,2,1,0:T(1,128)} %get-tuple-element.23), channel_id=1, source_target_pairs={{1,0},{2,1},{3,2},{4,3},{5,4},{6,5},{7,6},{8,7},{9,8},{10,9},{11,1... | collective-permute-start | bytes 589832 | tf_op jit(solution)/shard_map/ppermute | solution.py:19
  9.6 17.6 %all-to-all-start = ((s32[1,128,4]{2,0,1:T(1,128)}), s32[1,128,4]{2,0,1:T(1,128)}, u32[]{:S(2)}, u32[]{:S(2)}) async-start(s32[1,128,4]{2,0,1:T(1,128)} %copy.52), calls=%async_computation | async-start | bytes 131072 | tf_op jit(solution)/shard_map/all_to_all | solution.py:102
  20.8 8.9 %collective-permute-start.2 = (f32[2,1,18,1536]{3,2,1,0:T(8,128)}, f32[2,1,18,1536]{3,2,1,0:T(8,128)}, u32[]{:S(2)}, u32[]{:S(2)}) collective-permute-start(f32[2,1,18,1536]{3,2,1,0:T(8,128)} %get-tuple-element.20), channel_id=1, source_target_pairs={{0,16},{16,32},{32,48},{48,64},{64,80},{80,96},{96,112},{1,17},{17... | collective-permute-start | bytes 663560 | tf_op jit(solution)/shard_map/ppermute | solution.py:16
  24.4 8.4 %collective-permute-start.3 = (f32[2,1,18,1536]{3,2,1,0:T(8,128)}, f32[2,1,18,1536]{3,2,1,0:T(8,128)}, u32[]{:S(2)}, u32[]{:S(2)}) collective-permute-start(f32[2,1,18,1536]{3,2,1,0:T(8,128)} %get-tuple-element.21), channel_id=1, source_target_pairs={{16,0},{32,16},{48,32},{64,48},{80,64},{96,80},{112,96},{17,1},{33... | collective-permute-start | bytes 663560 | tf_op jit(solution)/shard_map/ppermute | solution.py:19
  34.8 0.7 copy-start.11
  35.5 3.5 %slice-start = ((s8[9437184]{0:T(1024)(128)(4,1)}), s8[4194304]{0:T(1024)(128)(4,1)S(1)}, s32[]{:S(2)}) async-start(s8[9437184]{0:T(1024)(128)(4,1)} %bitcast.75), calls=%async_computation.3 | async-start | bytes 8388608
  35.5 3.5 %slice-start.1 = ((s8[9437184]{0:T(1024)(128)(4,1)}), s8[4194304]{0:T(1024)(128)(4,1)S(1)}, s32[]{:S(2)}) async-start(s8[9437184]{0:T(1024)(128)(4,1)} %bitcast.75), calls=%async_computation.4 | async-start | bytes 8388608
  37.3 2.1 slice-start.2
  60.7 9.2 %copy-start.12 = (s32[1,128,4,4]{1,3,2,0:T(4,128)S(1)}, s32[1,128,4,4]{1,3,2,0:T(4,128)}, u32[]{:S(2)}) copy-start(s32[1,128,4,4]{1,3,2,0:T(4,128)} %param.19) | copy-start | bytes 24580
  60.7 33.3 %all-to-all-start.1 = ((bf16[128,1,4,1536]{3,2,1,0:T(4,128)(2,1)}), bf16[128,1,4,1536]{3,2,1,0:T(4,128)(2,1)S(1)}, u32[]{:S(2)}, u32[]{:S(2)}) async-start(bf16[128,1,4,1536]{3,2,1,0:T(4,128)(2,1)} %bitcast.62), calls=%async_computation.1 | async-start | bytes 3145728 | tf_op jit(solution)/shard_map/all_to_all | solution.py:104
  94.1 20.8 %copy-start.13 = (f32[1,128,4,4]{1,3,2,0:T(4,128)S(1)}, f32[1,128,4,4]{1,3,2,0:T(4,128)}, u32[]{:S(2)}) copy-start(f32[1,128,4,4]{1,3,2,0:T(4,128)} %param.20) | copy-start | bytes 24580
  94.1 20.8 %copy-start.15 = (f32[1,128,4]{1,2,0:T(4,128)S(1)}, f32[1,128,4]{1,2,0:T(4,128)}, u32[]{:S(2)}) copy-start(f32[1,128,4]{1,2,0:T(4,128)} %param.21) | copy-start | bytes 6148
  94.1 20.8 %copy-start.16 = (s32[1,128]{1,0:T(1,128)S(1)}, s32[1,128]{1,0:T(1,128)}, u32[]{:S(2)}) copy-start(s32[1,128]{1,0:T(1,128)} %param.18) | copy-start | bytes 1540
  119.8 46.7 %all-to-all-start.2 = ((f32[1,128,4,1536]{3,2,0,1:T(4,128)}), f32[1,128,4,1536]{3,2,0,1:T(4,128)}, u32[]{:S(2)}, u32[]{:S(2)}) async-start(f32[1,128,4,1536]{3,2,0,1:T(4,128)} %select_add_fusion), calls=%async_computation.2 | async-start | bytes 6291456 | tf_op jit(solution)/shard_map/all_to_all | solution.py:112
  190.1 13.0 %copy-start.2 = (f32[16,16,1536]{2,1,0:T(8,128)S(1)}, f32[16,16,1536]{2,1,0:T(8,128)}, u32[]{:S(2)}) copy-start(f32[16,16,1536]{2,1,0:T(8,128)} %param.13) | copy-start | bytes 4718596
  190.2 7.2 %collective-permute-start.4 = (f32[1,16,1,1536]{3,2,1,0:T(1,128)S(1)}, f32[1,16,1,1536]{3,2,1,0:T(1,128)S(1)}, u32[]{:S(2)}, u32[]{:S(2)}) collective-permute-start(f32[1,16,1,1536]{3,2,1,0:T(1,128)S(1)} %get-tuple-element.26), channel_id=1, source_target_pairs={{0,1},{1,2},{2,3},{3,4},{4,5},{5,6},{6,7},{7,8},{8,9},{9,10},{10,1... | collective-permute-start | bytes 294920 | tf_op jit(solution)/shard_map/ppermute | solution.py:16
  190.7 6.8 %collective-permute-start.5 = (f32[1,16,1,1536]{3,2,1,0:T(1,128)S(1)}, f32[1,16,1,1536]{3,2,1,0:T(1,128)S(1)}, u32[]{:S(2)}, u32[]{:S(2)}) collective-permute-start(f32[1,16,1,1536]{3,2,1,0:T(1,128)S(1)} %get-tuple-element.27), channel_id=1, source_target_pairs={{1,0},{2,1},{3,2},{4,3},{5,4},{6,5},{7,6},{8,7},{9,8},{10,9},{11,1... | collective-permute-start | bytes 294920 | tf_op jit(solution)/shard_map/ppermute | solution.py:19
  197.5 6.6 %collective-permute-start.6 = (f32[1,1,18,1536]{3,2,1,0:T(8,128)S(1)}, f32[1,1,18,1536]{3,2,1,0:T(8,128)S(1)}, u32[]{:S(2)}, u32[]{:S(2)}) collective-permute-start(f32[1,1,18,1536]{3,2,1,0:T(8,128)S(1)} %get-tuple-element.24), channel_id=1, source_target_pairs={{0,16},{16,32},{32,48},{48,64},{64,80},{80,96},{96,112},{1,17},{17... | collective-permute-start | bytes 331784 | tf_op jit(solution)/shard_map/ppermute | solution.py:16
  201.1 6.5 %collective-permute-start.7 = (f32[1,1,18,1536]{3,2,1,0:T(8,128)S(1)}, f32[1,1,18,1536]{3,2,1,0:T(8,128)S(1)}, u32[]{:S(2)}, u32[]{:S(2)}) collective-permute-start(f32[1,1,18,1536]{3,2,1,0:T(8,128)S(1)} %get-tuple-element.25), channel_id=1, source_target_pairs={{16,0},{32,16},{48,32},{64,48},{80,64},{96,80},{112,96},{17,1},{33... | collective-permute-start | bytes 331784 | tf_op jit(solution)/shard_map/ppermute | solution.py:19
  204.1 3.9 %copy-start.3 = (f32[256,1536]{1,0:T(8,128)S(1)}, f32[256,1536]{1,0:T(8,128)}, u32[]{:S(2)}) copy-start(f32[256,1536]{1,0:T(8,128)} %scatter_custom_fusion) | copy-start | bytes 4718596
  (7 other events, 5.0 us)
where the time goes:
time: 281 us; the launch traced here: 280 us
  waiting for transfers between devices  71.6 us (25%)
  blocking collectives  65 us (23%)
  starting transfers between devices  44.9 us (16%)
  local copies, waits for them, and re-layouts  39.5 us (14%)
  other arithmetic  31.8 us (11%)
  matrix products  25.1 us (9%)
    psum x1, blocking collectives, shards(): norm_sq = lax.psum(jnp.sum(residual * residual), ('band', 'sector'))  65 us
    all_to_all x1, waiting for transfers between devices, shards(): lax.all_to_all(row_grad, ('band', 'sector'), split_axis=1, concat_axis=0,...  38.6 us
    all_to_all x1, waiting for transfers between devices, shards(): lax.all_to_all(fetched, ('band', 'sector'), split_axis=0, concat_axis=1,...  23.2 us
    gather x5, local copies, waits for them, and re-layouts, shards(): sampled = jnp.take_along_axis(arrived, obs_pos, axis=3).astype(jnp.float32)  21.2 us
    ppermute x4, starting transfers between devices, padded_2(): lax.ppermute(lax.slice_in_dim(block, 0, width, axis=dim), axis, backward)  11.9 us
    dot_general x1, matrix products, shards(): jnp.dot(grad_act, w_in.T, preferred_element_type=jnp.float32)  10.6 us
    dot_general x1, matrix products, shards(): jnp.dot(tangent_hidden, w_out, preferred_element_type=jnp.float32)  10.3 us
    ppermute x4, starting transfers between devices, padded_2(): lax.ppermute(lax.slice_in_dim(block, block.shape[dim] - width, None, axis...  9.8 us
  transfers between devices with their start and end apart: 11, of which 6 were waited for; matrix products, arithmetic and copies ran while one was open for 4% of the time, Pallas kernels for 0%

commit v1 on v0

v1 whole, which is shorter than its diff:
```python
import functools
import math

import jax
import jax.numpy as jnp
from jax import lax
from jax.experimental import pallas as pl
from jax.experimental.pallas import tpu as pltpu
from jax.sharding import PartitionSpec as P

MESH = pl.DeviceIdType.MESH
F32 = jnp.float32
BF16 = jnp.bfloat16
LANES = 128


def gelu_slope(preact):
    normal_cdf = 0.5 * (1.0 + lax.erf(preact * (1.0 / math.sqrt(2.0))))
    normal_pdf = jnp.exp(-0.5 * preact * preact) * (1.0 / math.sqrt(2.0 * math.pi))
    return normal_cdf + preact * normal_pdf


def nn(left, right):
    return jnp.dot(left, right, preferred_element_type=F32)


def nt(left, right):
    return lax.dot_general(left, right, (((1,), (1,)), ((), ())), preferred_element_type=F32)


def tn(left, right):
    return lax.dot_general(left, right, (((0,), (0,)), ((), ())), preferred_element_type=F32)


def fold_lanes(values):
    total = values[:, :LANES]
    for at in range(LANES, values.shape[1], LANES):
        total = total + values[:, at : at + LANES]
    return total


def stencil_rows(row, west, east, corners, coef, lat_n, lon_n):
    width = west.shape[1]
    lat_at = lax.broadcasted_iota(jnp.int32, (lat_n, width), 0)
    lon_at = lax.broadcasted_iota(jnp.int32, (lon_n, width), 0)

    def column(mid, above, below, b):
        prev = jnp.where(lat_at == 0, above, pltpu.roll(mid, 1, 0))
        following = jnp.where(lat_at == lat_n - 1, below, pltpu.roll(mid, lat_n - 1, 0))
        return coef[b] * prev + coef[3 + b] * mid + coef[6 + b] * following

    rim_w = column(west, corners[0], corners[2], 0)
    rim_e = column(east, corners[1], corners[3], 2)
    rows = [row(-1), row(0)]
    for i in range(lat_n):
        rows.append(row(i + 1))
        part = [
            coef[b] * rows[i] + coef[3 + b] * rows[i + 1] + coef[6 + b] * rows[i + 2]
            for b in range(3)
        ]
        low = jnp.where(lon_at == 0, rim_w[i : i + 1], pltpu.roll(part[0], 1, 0))
        high = jnp.where(lon_at == lon_n - 1, rim_e[i : i + 1], pltpu.roll(part[2], lon_n - 1, 0))
        yield low + part[1] + high


def kernel(
    sizes,
    base_h, dir_h, res_h, coef_h, win_h, wout_h, patch_h, count_h, pos_h, wgt_h, rinv_h,
    out_ref,
    base, direc, res, coef, win, wout, patch, count, pos, wgt, rinv,
    mixed, slopes, hidden, tang, weights, onehot, spread, obs, obs_b, gmix,
    fedge_s, fedge_r, fcorn_s, fcorn_r, bedge_s, bedge_r, bcorn_s, bcorn_r,
    pay, a0, a1, a2, a3, red0, red1, red2,
    load_sem, win_sem, wout_sem,
    fs_sem, fr_sem, bs_sem, br_sem,
    p1s_sem, p1r_sem, p2s_sem, p2r_sem, r1s_sem, r1r_sem, r2s_sem, r2r_sem,
):
    nb, ns, lat_n, lon_n, feat, hid, slot_n, tap_n, n1, n2, nbk = sizes
    tok_n = lat_n * lon_n
    block_n = nb * ns
    b = lax.axis_index("band")
    s = lax.axis_index("sector")

    def band(step):
        return lax.rem(b + step + nb, nb)

    def sector(step):
        return lax.rem(s + step + ns, ns)

    loads = {}
    pairs = dict(
        patch=(patch_h, patch), count=(count_h, count), pos=(pos_h, pos), wgt=(wgt_h, wgt),
        rinv=(rinv_h, rinv), coef=(coef_h, coef), dir=(dir_h, direc), base=(base_h, base),
    )
    for at, (name, (src, dst)) in enumerate(pairs.items()):
        loads[name] = pltpu.make_async_copy(src, dst, load_sem.at[at])
        loads[name].start()
    win_loads = []
    for at in range(hid // n1):
        cols = pl.ds(at * n1, n1)
        win_loads.append(pltpu.make_async_copy(win_h.at[:, cols], win.at[:, cols], win_sem.at[at]))
        win_loads[-1].start()
    loads["res"] = pltpu.make_async_copy(res_h, res, load_sem.at[8])
    loads["res"].start()
    wout_loads = []
    for at in range(feat // n2):
        cols = pl.ds(at * n2, n2)
        wout_loads.append(pltpu.make_async_copy(wout_h.at[:, cols], wout.at[:, cols], wout_sem.at[at]))
        wout_loads[-1].start()

    diagonal = [(band(db), sector(ds)) for db in (1, -1) for ds in (1, -1)]
    partners = [(band(d), s) for d in range(1, nb)] + [(b, sector(d)) for d in range(1, ns)] + diagonal
    barrier = pltpu.get_barrier_semaphore()
    for partner in partners:
        pl.semaphore_signal(barrier, inc=1, device_id=partner, device_id_type=MESH)

    def send(src, dst, send_sem, recv_sem, to):
        copy = pltpu.make_async_remote_copy(
            src_ref=src, dst_ref=dst, send_sem=send_sem, recv_sem=recv_sem,
            device_id=to, device_id_type=MESH,
        )
        return copy

    edge_to = [(band(1), s), (band(-1), s), (b, sector(1)), (b, sector(-1))]
    corner_to = [
        (band(1), sector(1)), (band(1), sector(-1)), (band(-1), sector(1)), (band(-1), sector(-1)),
    ]
    last_i, last_j = lat_n - 1, lon_n - 1

    for name in ("dir", "base"):
        loads[name].wait()
    for at, field in enumerate((base, direc)):
        for side, rim in enumerate((field[last_i], field[0], field[:, last_j], field[:, 0])):
            fedge_s[side, at] = rim.astype(BF16)
        for side, (ci, cj) in enumerate(((last_i, last_j), (last_i, 0), (0, last_j), (0, 0))):
            fcorn_s[side, at : at + 1] = field[ci, cj : cj + 1]
    pl.semaphore_wait(barrier, len(partners))
    fwd = []
    for side in range(4):
        fwd.append(send(fedge_s.at[side], fedge_r.at[side], fs_sem.at[side], fr_sem.at[side], edge_to[side]))
        fwd[-1].start()
    for side in range(4):
        fwd.append(
            send(fcorn_s.at[side], fcorn_r.at[side], fs_sem.at[4 + side], fr_sem.at[4 + side], corner_to[side])
        )
        fwd[-1].start()

    for name in ("patch", "count", "pos", "wgt", "rinv"):
        loads[name].wait()
    slot_at = lax.broadcasted_iota(jnp.int32, (slot_n, block_n), 0)
    tap_all = slot_n * tap_n
    pay[...] = jnp.zeros_like(pay)
    pay[0:slot_n] = patch[...].astype(F32)
    pay[slot_n : 2 * slot_n] = jnp.where(slot_at < count[...], rinv[...], 0.0)
    pay[2 * slot_n : 2 * slot_n + tap_all] = pos[...].astype(F32)
    pay[2 * slot_n + tap_all : 2 * slot_n + 2 * tap_all] = wgt[...]
    a0[...] = jnp.transpose(pay[...]).reshape(nb, ns, LANES)
    a1[b] = a0[b]
    phase1 = []
    for d in range(1, nb):
        phase1.append(send(a0.at[band(d)], a1.at[b], p1s_sem.at[d - 1], p1r_sem.at[d - 1], (band(d), s)))
        phase1[-1].start()

    loads["res"].wait()
    norm = jnp.zeros((lon_n, LANES), F32)
    grow = jnp.zeros((lon_n, LANES), F32)

    def square(i, carry):
        norm, grow = carry
        r, d = res[i], direc[i]
        return norm + fold_lanes(r * r), grow + fold_lanes(d * d)

    norm, grow = lax.fori_loop(0, lat_n, square, (norm, grow))
    red0[0:1] = jnp.sum(norm, axis=0, keepdims=True)
    red0[1:2] = jnp.sum(grow, axis=0, keepdims=True)

    loads["coef"].wait()
    for copy in fwd:
        copy.wait_recv()
    north = (b > 0).astype(F32)
    south = (b < nb - 1).astype(F32)
    cw = 256

    def mix(k, carry):
        cols = pl.ds(pl.multiple_of(k * cw, cw), cw)
        taps = [coef[t : t + 1, cols] for t in range(9)]
        for at, field in enumerate((base, direc)):
            def row(r):
                if r < 0:
                    return fedge_r[0, at, :, cols].astype(F32) * north
                if r == lat_n:
                    return fedge_r[1, at, :, cols].astype(F32) * south
                return field[r, :, cols]

            corners = [
                fcorn_r[side, at : at + 1, cols] * (north if side < 2 else south) for side in range(4)
            ]
            west = fedge_r[2, at, :, cols].astype(F32)
            east = fedge_r[3, at, :, cols].astype(F32)
            for i, summed in enumerate(stencil_rows(row, west, east, corners, taps, lat_n, lon_n)):
                start = at * tok_n + i * lon_n
                mixed[start : start + lon_n, cols] = summed.astype(BF16)
        return carry

    lax.fori_loop(0, feat // cw, mix, 0)

    phase2 = []
    for n in range(hid // n1):
        win_loads[n].wait()
        cols = slice(n * n1, (n + 1) * n1)
        both = nn(mixed[...], win[:, cols])
        slope = gelu_slope(both[:tok_n])
        slopes[:, cols] = slope
        hidden[:, cols] = (slope * both[tok_n:]).astype(BF16)
        if n == 1:
            for copy in phase1:
                copy.wait_recv()
            for q in range(ns):
                a2[q] = a1[:, q, :]
            a3[s] = a2[s]
            for d in range(1, ns):
                phase2.append(
                    send(a2.at[sector(d)], a3.at[s], p2s_sem.at[d - 1], p2r_sem.at[d - 1], (b, sector(d)))
                )
                phase2[-1].start()
        if n == hid // n1 - 2:
            for copy in phase2:
                copy.wait_recv()

    stations = slot_n * block_n
    told = a3[...].reshape(block_n, LANES)
    cell_at = lax.broadcasted_iota(jnp.int32, (block_n, tok_n), 1).astype(F32)
    for c in range(slot_n):
        onehot[c * block_n : (c + 1) * block_n] = jnp.where(told[:, c : c + 1] == cell_at, 1.0, 0.0).astype(BF16)
    rb = min(32, block_n)
    lane_at = lax.broadcasted_iota(jnp.int32, (rb, LANES), 1).astype(F32)
    for c in range(slot_n):
        for r in range(0, block_n, rb):
            rows = told[r : r + rb]
            first = 2 * slot_n + c * tap_n
            chans = [jnp.broadcast_to(rows[:, first + k : first + k + 1], (rb, LANES)) for k in range(tap_n)]
            first += tap_all
            wgts = [jnp.broadcast_to(rows[:, first + k : first + k + 1], (rb, LANES)) for k in range(tap_n)]
            for j in range(feat // LANES):
                here = lane_at + float(j * LANES)
                summed = jnp.where(chans[0] == here, wgts[0], 0.0)
                for k in range(1, tap_n):
                    summed = summed + jnp.where(chans[k] == here, wgts[k], 0.0)
                weights[c * block_n + r : c * block_n + r + rb, j * LANES : (j + 1) * LANES] = summed

    seen = jnp.zeros((stations, LANES), F32)
    for n in range(feat // n2):
        wout_loads[n].wait()
        cols = slice(n * n2, (n + 1) * n2)
        own = direc[:, :, cols].reshape(tok_n, n2)
        tang[:, cols] = (own + nn(hidden[...], wout[:, cols])).astype(BF16)
        sampled = nn(onehot[...], tang[:, cols])
        seen = seen + fold_lanes(sampled * weights[:, cols])
    misfit = jnp.sum(seen, axis=1, keepdims=True)
    inverse = jnp.concatenate([told[:, slot_n + c : slot_n + c + 1] for c in range(slot_n)], axis=0)
    scaled = inverse * misfit
    lane0 = lax.broadcasted_iota(jnp.int32, (1, LANES), 1) == 0
    red0[1:2] = red0[1:2] + jnp.where(lane0, jnp.sum(scaled * misfit, axis=0, keepdims=True), 0.0)

    reduce1 = []
    red1[b] = red0[...]
    for d in range(1, nb):
        reduce1.append(send(red0, red1.at[b], r1s_sem.at[d - 1], r1r_sem.at[d - 1], (band(d), s)))
        reduce1[-1].start()

    for n in range(feat // n2):
        cols = slice(n * n2, (n + 1) * n2)
        deposit = scaled * weights[:, cols]
        rough = deposit.astype(BF16)
        fine = (deposit - rough.astype(F32)).astype(BF16)
        summed = tn(onehot[...], rough) + tn(onehot[...], fine)
        obs[:, cols] = summed
        obs_b[:, cols] = summed.astype(BF16)

    for n in range(hid // n1):
        rows = slice(n * n1, (n + 1) * n1)
        hidden[:, rows] = (slopes[:, rows] * nt(obs_b[...], wout[rows, :])).astype(BF16)

    for copy in reduce1:
        copy.wait_recv()
    total = red1[0]
    for d in range(1, nb):
        total = total + red1[d]
    red0b = red2.at[s]
    red0b[...] = total
    reduce2 = []
    for d in range(1, ns):
        reduce2.append(send(red2.at[s], red2.at[s], r2s_sem.at[d - 1], r2r_sem.at[d - 1], (b, sector(d))))
        reduce2[-1].start()

    bwd = []
    for n in range(feat // nbk):
        rows = slice(n * nbk, (n + 1) * nbk)
        part = nt(hidden[...], win[rows, :]).reshape(lat_n, lon_n, nbk)
        gmix[:, :, rows] = part
        for side, rim in enumerate(
            (gmix[last_i, :, rows], gmix[0, :, rows], gmix[:, last_j, rows], gmix[:, 0, rows])
        ):
            bedge_s[n, side] = rim.astype(BF16)
        for side, (ci, cj) in enumerate(((last_i, last_j), (last_i, 0), (0, last_j), (0, 0))):
            bcorn_s[n, side] = gmix[ci, cj : cj + 1, rows]
        sent = []
        for side in range(4):
            sent.append(
                send(
                    bedge_s.at[n, side], bedge_r.at[n, side],
                    bs_sem.at[n, side], br_sem.at[n, side], edge_to[side],
                )
            )
        for side in range(4):
            sent.append(
                send(
                    bcorn_s.at[n, side], bcorn_r.at[n, side],
                    bs_sem.at[n, 4 + side], br_sem.at[n, 4 + side], corner_to[side],
                )
            )
        for copy in sent:
            copy.start()
        bwd.append(sent)

    for copy in reduce2:
        copy.wait_recv()
    total = red2[0]
    for d in range(1, ns):
        total = total + red2[d]
    total = jnp.sum(total, axis=1, keepdims=True)
    alpha = total[0:1] / total[1:2]

    for n in range(feat // nbk):
        for copy in bwd[n]:
            copy.wait_recv()

        def unmix(k, carry):
            cols = pl.ds(pl.multiple_of(n * nbk + k * cw, cw), cw)
            inner = pl.ds(pl.multiple_of(k * cw, cw), cw)
            taps = [coef[8 - t : 9 - t, cols] for t in range(9)]

            def row(r):
                if r < 0:
                    return bedge_r[n, 0, :, inner].astype(F32) * north
                if r == lat_n:
                    return bedge_r[n, 1, :, inner].astype(F32) * south
                return gmix[r, :, cols]

            corners = [bcorn_r[n, side, :, inner] * (north if side < 2 else south) for side in range(4)]
            west = bedge_r[n, 2, :, inner].astype(F32)
            east = bedge_r[n, 3, :, inner].astype(F32)
            for i, summed in enumerate(stencil_rows(row, west, east, corners, taps, lat_n, lon_n)):
                hess = direc[i, :, cols] + obs[i * lon_n : (i + 1) * lon_n, cols] + summed
                out_ref[i, :, cols] = res[i, :, cols] - alpha * hess
            return carry

        lax.fori_loop(0, nbk // cw, unmix, 0)

    for copy in fwd + phase1 + phase2 + reduce1 + reduce2 + [copy for sent in bwd for copy in sent]:
        copy.wait_send()


def shards(
    nb, ns,
    base_state, direction, residual, mix_coef, w_in, w_out,
    obs_patch, obs_count, obs_pos, obs_wgt, obs_rinv,
):
    lat_n, lon_n, feat = base_state.shape
    hid = w_in.shape[1]
    slot_n, tap_n = obs_pos.shape[2:]
    tok_n = lat_n * lon_n
    block_n = nb * ns
    n1 = min(512, hid)
    n2 = min(512, feat)
    nbk = min(512, feat)
    patch = obs_patch[0].T
    count = obs_count
    pos = jnp.transpose(obs_pos[0], (1, 2, 0)).reshape(slot_n * tap_n, block_n)
    wgt = jnp.transpose(obs_wgt[0], (1, 2, 0)).reshape(slot_n * tap_n, block_n)
    rinv = obs_rinv[0].T
    stations = slot_n * block_n
    dma = pltpu.SemaphoreType.DMA
    vmem = pltpu.VMEM
    chunks = feat // nbk
    scratch = [
        vmem((lat_n, lon_n, feat), F32), vmem((lat_n, lon_n, feat), F32), vmem((lat_n, lon_n, feat), F32),
        vmem(mix_coef.shape, F32), vmem(w_in.shape, BF16), vmem(w_out.shape, BF16),
        vmem(patch.shape, jnp.int32), vmem(count.shape, jnp.int32), vmem(pos.shape, jnp.int32),
        vmem(wgt.shape, F32), vmem(rinv.shape, F32),
        vmem((2 * tok_n, feat), BF16), vmem((tok_n, hid), F32), vmem((tok_n, hid), BF16),
        vmem((tok_n, feat), BF16), vmem((stations, feat), F32), vmem((stations, tok_n), BF16),
        vmem((8, LANES), F32), vmem((tok_n, feat), F32), vmem((tok_n, feat), BF16),
        vmem((lat_n, lon_n, feat), F32),
        vmem((4, 2, 16, feat), BF16), vmem((4, 2, 16, feat), BF16),
        vmem((4, 2, feat), F32), vmem((4, 2, feat), F32),
        vmem((chunks, 4, 16, nbk), BF16), vmem((chunks, 4, 16, nbk), BF16),
        vmem((chunks, 4, 1, nbk), F32), vmem((chunks, 4, 1, nbk), F32),
        vmem((LANES, block_n), F32), vmem((nb, ns, LANES), F32), vmem((nb, ns, LANES), F32),
        vmem((ns, nb, LANES), F32), vmem((ns, nb, LANES), F32),
        vmem((2, LANES), F32), vmem((nb, 2, LANES), F32), vmem((ns, 2, LANES), F32),
        dma((9,)), dma((hid // n1,)), dma((feat // n2,)),
        dma((8,)), dma((8,)), dma((chunks, 8)), dma((chunks, 8)),
        dma((nb - 1,)), dma((nb - 1,)), dma((ns - 1,)), dma((ns - 1,)),
        dma((nb - 1,)), dma((nb - 1,)), dma((ns - 1,)), dma((ns - 1,)),
    ]
    sizes = (nb, ns, lat_n, lon_n, feat, hid, slot_n, tap_n, n1, n2, nbk)
    return pl.pallas_call(
        functools.partial(kernel, sizes),
        out_shape=jax.ShapeDtypeStruct(base_state.shape, F32),
        in_specs=[pl.BlockSpec(memory_space=pl.ANY)] * 11,
        out_specs=pl.BlockSpec(memory_space=pltpu.VMEM),
        scratch_shapes=scratch,
        compiler_params=pltpu.CompilerParams(
            collective_id=0, has_side_effects=True, vmem_limit_bytes=60 * 2**20
        ),
    )(base_state, direction, residual, mix_coef, w_in, w_out, patch, count, pos, wgt, rinv)


def solution(mesh):
    return jax.shard_map(
        functools.partial(shards, mesh.shape["band"], mesh.shape["sector"]),
        mesh=mesh,
        in_specs=(
            P("band", "sector", None),
            P("band", "sector", None),
            P("band", "sector", None),
            P(),
            P(),
            P(),
            P(("band", "sector"), None, None),
            P(("band", "sector"), None),
            P(("band", "sector"), None, None, None),
            P(("band", "sector"), None, None, None),
            P(("band", "sector"), None, None),
        ),
        out_specs=P("band", "sector", None),
        check_vma=False,
    )
```

time: 281 us -> 51.4 us (0.18)
  waiting for transfers between devices: 71.6 us -> 0 us
  blocking collectives: 65 us -> 0 us
  Pallas kernels: 0 us -> 48.6 us
  starting transfers between devices: 44.9 us -> 0 us
  local copies, waits for them, and re-layouts: 39.5 us -> 2.69 us
  other arithmetic: 31.8 us -> 0 us
  matrix products: 25.1 us -> 0 us
    psum x1 -> x0, blocking collectives: 65 us -> none  [shards(): norm_sq = lax.psum(jnp.sum(residual * residual), ('band', 'sector'))]
    all_to_all x3 -> x0, waiting for transfers between devices: 62.6 us -> none  [the longest x1 38.6 us: shards(): lax.all_to_all(row_grad, ('band', 'sector'), split_axis=1, concat_axis=0,...]
    pallas_call x0 -> x1, Pallas kernels: none -> 48.6 us  [shards(): pl.pallas_call(functools.partial(kernel, sizes), out_shape=jax.ShapeDtype...]
    gather x7 -> x0, local copies, waits for them, and re-layouts: 28 us -> none  [the longest x5 21.2 us: shards(): sampled = jnp.take_along_axis(arrived, obs_pos, axis=3).astype(jnp.float32)]
    dot_general x3 -> x0, matrix products: 25.1 us -> none  [the longest x1 10.6 us: shards(): jnp.dot(grad_act, w_in.T, preferred_element_type=jnp.float32)]
    all_to_all x3 -> x0, starting transfers between devices: 23.2 us -> none  [the longest x1 9.18 us: shards(): lax.all_to_all(fetched, ('band', 'sector'), split_axis=0, concat_axis=1,...]
    ppermute x8 -> x0, starting transfers between devices: 21.7 us -> none  [the longest x4 11.9 us: padded_2(): lax.ppermute(lax.slice_in_dim(block, 0, width, axis=dim), axis, backward)]
    ppermute x8 -> x0, waiting for transfers between devices: 9 us -> none  [the longest x4 6.6 us: padded_2(): lax.ppermute(lax.slice_in_dim(block, 0, width, axis=dim), axis, backward)]
  transfers between devices with their start and end apart: 11 -> 0, of which waited for: 6 -> 0; matrix products, arithmetic and copies ran while one was open for 4% -> 0% of each run, Pallas kernels for 0% -> 0%
where the time goes in v1:
time: 51.4 us; the launch traced here: 51.3 us
  Pallas kernels  48.6 us (95%)
  local copies, waits for them, and re-layouts  2.69 us (5%)
    pallas_call x1, Pallas kernels, shards(): pl.pallas_call(functools.partial(kernel, sizes), out_shape=jax.ShapeDtype...  48.6 us
    unnamed x1, local copies, waits for them, and re-layouts  2.69 us

profile of v1, /device:TPU:1, one launch (start us, length us, event | category | flops | bytes accessed | tf_op | source)
XLA Modules:
  0.0 51.3 jit_solution(15786007995570965007)
XLA Ops:
  0.0 48.6 %shard_map.109 = f32[16,16,1536]{2,1,0:T(8,128)} custom-call(f32[16,16,1536]{2,1,0:T(8,128)} %base_h.1, f32[16,16,1536]{2,1,0:T(8,128)} %dir_h.1, f32[16,16,1536]{2,1,0:T(8,128)} %res_h.1, f32[9,1536]{1,0:T(8,128)} %coef_h.1, bf16[1536,3072]{1,0:T(8,128)(2,1)} %win_h.1, bf16[3072,1536]{1,0:T(8,128)(2,1)} %wout_h.1, s32[4,128]{1,0:T(4,128)} %bitcast.18, ...), custom_call_target="tpu_custom_call" | custom-call | tf_op jit(solution)/shard_map/pallas_call | solution.py:408
  48.6 2.7 %copy.13 = f32[16,16,1536]{2,1,0:T(8,128)} copy(f32[16,16,1536]{2,1,0:T(8,128)} %shard_map.109) | data formatting | bytes 3145728

commit v2 on v1

v2 whole, which is shorter than its diff:
```python
import functools
import math

import jax
import jax.numpy as jnp
from jax import lax
from jax.experimental import pallas as pl
from jax.experimental.pallas import tpu as pltpu
from jax.sharding import PartitionSpec as P

MESH = pl.DeviceIdType.MESH
F32 = jnp.float32
BF16 = jnp.bfloat16
LANES = 128


def gelu_slope(preact):
    normal_cdf = 0.5 * (1.0 + lax.erf(preact * (1.0 / math.sqrt(2.0))))
    normal_pdf = jnp.exp(-0.5 * preact * preact) * (1.0 / math.sqrt(2.0 * math.pi))
    return normal_cdf + preact * normal_pdf


def nn(left, right):
    return jnp.dot(left, right, preferred_element_type=F32)


def nt(left, right):
    return lax.dot_general(left, right, (((1,), (1,)), ((), ())), preferred_element_type=F32)


def tn(left, right):
    return lax.dot_general(left, right, (((0,), (0,)), ((), ())), preferred_element_type=F32)


def fold_lanes(values):
    total = values[:, :LANES]
    for at in range(LANES, values.shape[1], LANES):
        total = total + values[:, at : at + LANES]
    return total


def shifted(part, lon_n):
    lon_at = lax.broadcasted_iota(jnp.int32, part[0].shape, 0)
    low = jnp.where(lon_at == 0, 0.0, pltpu.roll(part[0], 1, 0))
    high = jnp.where(lon_at == lon_n - 1, 0.0, pltpu.roll(part[2], lon_n - 1, 0))
    return low + part[1] + high


def inner_rows(row, coef, lat_n, lon_n):
    before, now = None, row(0)
    for i in range(lat_n):
        after = row(i + 1) if i < lat_n - 1 else None
        part = []
        for b in range(3):
            summed = coef[3 + b] * now
            if before is not None:
                summed = summed + coef[b] * before
            if after is not None:
                summed = summed + coef[6 + b] * after
            part.append(summed)
        yield shifted(part, lon_n)
        before, now = now, after


def rim_rows(north, south, west, east, corners, coef, lat_n, lon_n):
    width = west.shape[1]
    lat_at = lax.broadcasted_iota(jnp.int32, (lat_n, width), 0)
    lon_at = lax.broadcasted_iota(jnp.int32, (lon_n, width), 0)

    def column(mid, above, below, b):
        prev = jnp.where(lat_at == 0, above, pltpu.roll(mid, 1, 0))
        following = jnp.where(lat_at == lat_n - 1, below, pltpu.roll(mid, lat_n - 1, 0))
        return coef[b] * prev + coef[3 + b] * mid + coef[6 + b] * following

    rim_w = column(west, corners[0], corners[2], 0)
    rim_e = column(east, corners[1], corners[3], 2)
    for i in range(lat_n):
        rim = jnp.where(lon_at == 0, rim_w[i : i + 1], 0.0) + jnp.where(lon_at == lon_n - 1, rim_e[i : i + 1], 0.0)
        if i == 0:
            rim = rim + shifted([coef[b] * north for b in range(3)], lon_n)
        if i == lat_n - 1:
            rim = rim + shifted([coef[6 + b] * south for b in range(3)], lon_n)
        yield rim


def kernel(
    sizes,
    base_h, dir_h, res_h, coef_h, win_h, wout_h, patch_h, count_h, pos_h, wgt_h, rinv_h,
    out_ref,
    base, direc, res, coef, win, wout, patch, count, pos, wgt, rinv,
    acc, mixed, slopes, hidden, tang, weights, onehot, obs, obs_b, gmix,
    fedge_s, fedge_r, fcorn_s, fcorn_r, bedge_s, bedge_r, bcorn_s, bcorn_r,
    pay, a0, a1, a2, a3, red0, red1, red2,
    load_sem, fs_sem, fr_sem, bs_sem, br_sem,
    p1s_sem, p1r_sem, p2s_sem, p2r_sem, r1s_sem, r1r_sem, r2s_sem, r2r_sem,
):
    nb, ns, lat_n, lon_n, feat, hid, slot_n, tap_n, n1, n2, nbk, cw = sizes
    tok_n = lat_n * lon_n
    block_n = nb * ns
    last_i, last_j = lat_n - 1, lon_n - 1
    b = lax.axis_index("band")
    s = lax.axis_index("sector")

    def band(step):
        return lax.rem(b + step + nb, nb)

    def sector(step):
        return lax.rem(s + step + ns, ns)

    edge_to = [(band(1), s), (band(-1), s), (b, sector(1)), (b, sector(-1))]
    corner_to = [
        (band(1), sector(1)), (band(1), sector(-1)), (band(-1), sector(1)), (band(-1), sector(-1)),
    ]
    partners = [(band(d), s) for d in range(1, nb)] + [(b, sector(d)) for d in range(1, ns)] + corner_to
    barrier = pltpu.get_barrier_semaphore()
    for partner in partners:
        pl.semaphore_signal(barrier, inc=1, device_id=partner, device_id_type=MESH)

    loads = {}
    pairs = dict(
        base=(base_h, base), dir=(dir_h, direc),
        patch=(patch_h, patch), count=(count_h, count), pos=(pos_h, pos), wgt=(wgt_h, wgt), rinv=(rinv_h, rinv),
        coef=(coef_h, coef), win=(win_h, win), res=(res_h, res), wout=(wout_h, wout),
    )
    for at, (name, (src, dst)) in enumerate(pairs.items()):
        loads[name] = pltpu.make_async_copy(src, dst, load_sem.at[at])
        loads[name].start()

    def send(src, dst, send_sem, recv_sem, to):
        copy = pltpu.make_async_remote_copy(
            src_ref=src, dst_ref=dst, send_sem=send_sem, recv_sem=recv_sem, device_id=to, device_id_type=MESH
        )
        copy.start()
        return copy

    rim_at = ((last_i, last_j), (last_i, 0), (0, last_j), (0, 0))
    for at, (name, field) in enumerate((("base", base), ("dir", direc))):
        loads[name].wait()
        for side, rim in enumerate((field[last_i], field[0], field[:, last_j], field[:, 0])):
            fedge_s[at, side] = rim.astype(BF16)
        for side, (ci, cj) in enumerate(rim_at):
            fcorn_s[at, side] = field[ci, cj : cj + 1]
    pl.semaphore_wait(barrier, len(partners))
    fwd = []
    for at in range(2):
        sent = []
        for side in range(4):
            sent.append(
                send(
                    fedge_s.at[at, side], fedge_r.at[at, side],
                    fs_sem.at[at, side], fr_sem.at[at, side], edge_to[side],
                )
            )
        for side in range(4):
            sent.append(
                send(
                    fcorn_s.at[at, side], fcorn_r.at[at, side],
                    fs_sem.at[at, 4 + side], fr_sem.at[at, 4 + side], corner_to[side],
                )
            )
        fwd.append(sent)

    for name in ("patch", "count", "pos", "wgt", "rinv"):
        loads[name].wait()
    slot_at = lax.broadcasted_iota(jnp.int32, (slot_n, block_n), 0)
    tap_all = slot_n * tap_n
    pay[...] = jnp.zeros_like(pay)
    pay[0:slot_n] = patch[...].astype(F32)
    pay[slot_n : 2 * slot_n] = jnp.where(slot_at < count[...], rinv[...], 0.0)
    pay[2 * slot_n : 2 * slot_n + tap_all] = pos[...].astype(F32)
    pay[2 * slot_n + tap_all : 2 * slot_n + 2 * tap_all] = wgt[...]
    a0[...] = jnp.transpose(pay[...]).reshape(nb, ns, LANES)
    a1[b] = a0[b]
    phase1 = []
    for d in range(1, nb):
        phase1.append(send(a0.at[band(d)], a1.at[b], p1s_sem.at[d - 1], p1r_sem.at[d - 1], (band(d), s)))

    loads["coef"].wait()
    for at, field in enumerate((base, direc)):
        def premix(k, carry, at=at, field=field):
            cols = pl.ds(pl.multiple_of(k * cw, cw), cw)
            taps = [coef[t : t + 1, cols] for t in range(9)]
            for i, summed in enumerate(inner_rows(lambda r: field[r, :, cols], taps, lat_n, lon_n)):
                acc[at, i, :, cols] = summed
            return carry

        lax.fori_loop(0, feat // cw, premix, 0)

    loads["res"].wait()
    zero = jnp.zeros((lon_n, LANES), F32)

    def square(i, carry):
        norm, grow = carry
        r, d = res[i], direc[i]
        return norm + fold_lanes(r * r), grow + fold_lanes(d * d)

    norm, grow = lax.fori_loop(0, lat_n, square, (zero, zero))
    red0[0:1] = jnp.sum(norm, axis=0, keepdims=True)
    red0[1:2] = jnp.sum(grow, axis=0, keepdims=True)

    inside_n = (b > 0).astype(F32)
    inside_s = (b < nb - 1).astype(F32)

    def rims_in(edge, corn, taps, cols):
        corners = [corn.at[side][:, cols] * (inside_n if side < 2 else inside_s) for side in range(4)]
        north = edge.at[0][:, cols].astype(F32) * inside_n
        south = edge.at[1][:, cols].astype(F32) * inside_s
        west = edge.at[2][:, cols].astype(F32)
        east = edge.at[3][:, cols].astype(F32)
        return rim_rows(north, south, west, east, corners, taps, lat_n, lon_n)

    def postmix(at, cols):
        taps = [coef[t : t + 1, cols] for t in range(9)]
        for i, rim in enumerate(rims_in(fedge_r.at[at], fcorn_r.at[at], taps, cols)):
            start = at * tok_n + i * lon_n
            mixed[start : start + lon_n, cols] = (acc[at, i, :, cols] + rim).astype(BF16)

    for copy in fwd[0]:
        copy.wait_recv()

    def postmix_base(k, carry):
        postmix(0, pl.ds(pl.multiple_of(k * cw, cw), cw))
        return carry

    lax.fori_loop(0, feat // cw, postmix_base, 0)
    loads["win"].wait()

    phase2 = []
    posts = [slice(k * cw, (k + 1) * cw) for k in range(feat // cw)]
    half = hid // n1 // 2
    for n in range(hid // n1):
        cols = slice(n * n1, (n + 1) * n1)
        slopes[:, cols] = gelu_slope(nn(mixed[:tok_n], win[:, cols]))
        if n == 0:
            for copy in phase1:
                copy.wait_recv()
            for q in range(ns):
                a2[q] = a1[:, q, :]
            a3[s] = a2[s]
            for d in range(1, ns):
                phase2.append(
                    send(a2.at[sector(d)], a3.at[s], p2s_sem.at[d - 1], p2r_sem.at[d - 1], (b, sector(d)))
                )
        if n == half - 1:
            for copy in fwd[1]:
                copy.wait_recv()
        if n >= half:
            share = -(-len(posts) // (hid // n1 - half))
            for part in posts[(n - half) * share : (n - half + 1) * share]:
                postmix(1, part)

    stations = slot_n * block_n
    rb = min(32, block_n)
    blocks = [(c, r) for c in range(slot_n) for r in range(0, block_n, rb)]

    def place(c):
        told = a3[...].reshape(block_n, LANES)
        cell_at = lax.broadcasted_iota(jnp.int32, (block_n, tok_n), 1).astype(F32)
        onehot[c * block_n : (c + 1) * block_n] = jnp.where(told[:, c : c + 1] == cell_at, 1.0, 0.0).astype(BF16)

    def spread(c, r):
        rows = a3[r // nb : (r + rb) // nb].reshape(rb, LANES)
        lane_at = lax.broadcasted_iota(jnp.int32, (rb, LANES), 1).astype(F32)
        first = 2 * slot_n + c * tap_n
        chans = [jnp.broadcast_to(rows[:, first + k : first + k + 1], (rb, LANES)) for k in range(tap_n)]
        first += tap_all
        wgts = [jnp.broadcast_to(rows[:, first + k : first + k + 1], (rb, LANES)) for k in range(tap_n)]
        for j in range(feat // LANES):
            here = lane_at + float(j * LANES)
            summed = jnp.where(chans[0] == here, wgts[0], 0.0)
            for k in range(1, tap_n):
                summed = summed + jnp.where(chans[k] == here, wgts[k], 0.0)
            weights[c * block_n + r : c * block_n + r + rb, j * LANES : (j + 1) * LANES] = summed

    steps = hid // n1
    for n in range(steps):
        cols = slice(n * n1, (n + 1) * n1)
        hidden[:, cols] = (slopes[:, cols] * nn(mixed[tok_n:], win[:, cols])).astype(BF16)
        if n == half:
            for copy in phase2:
                copy.wait_recv()
            loads["wout"].wait()
        if n > half:
            share = -(-len(blocks) // (steps - half - 1))
            for c, r in blocks[(n - half - 1) * share : (n - half) * share]:
                spread(c, r)
    for c in range(slot_n):
        place(c)

    seen = jnp.zeros((stations, LANES), F32)
    for n in range(feat // n2):
        cols = slice(n * n2, (n + 1) * n2)
        own = direc[:, :, cols].reshape(tok_n, n2)
        tang[:, cols] = (own + nn(hidden[...], wout[:, cols])).astype(BF16)
        sampled = nn(onehot[...], tang[:, cols])
        seen = seen + fold_lanes(sampled * weights[:, cols])
    misfit = jnp.sum(seen, axis=1, keepdims=True)
    told = a3[...].reshape(block_n, LANES)
    inverse = jnp.concatenate([told[:, slot_n + c : slot_n + c + 1] for c in range(slot_n)], axis=0)
    scaled = inverse * misfit
    lane0 = lax.broadcasted_iota(jnp.int32, (1, LANES), 1) == 0
    red0[1:2] = red0[1:2] + jnp.where(lane0, jnp.sum(scaled * misfit, axis=0, keepdims=True), 0.0)

    reduce1 = []
    red1[b] = red0[...]
    for d in range(1, nb):
        reduce1.append(send(red0, red1.at[b], r1s_sem.at[d - 1], r1r_sem.at[d - 1], (band(d), s)))

    for n in range(feat // n2):
        cols = slice(n * n2, (n + 1) * n2)
        deposit = scaled * weights[:, cols]
        rough = deposit.astype(BF16)
        fine = (deposit - rough.astype(F32)).astype(BF16)
        summed = tn(onehot[...], rough) + tn(onehot[...], fine)
        obs[:, cols] = summed
        obs_b[:, cols] = summed.astype(BF16)

    reduce2 = []
    for n in range(hid // n1):
        rows = slice(n * n1, (n + 1) * n1)
        hidden[:, rows] = (slopes[:, rows] * nt(obs_b[...], wout[rows, :])).astype(BF16)
        if n == half - 1:
            for copy in reduce1:
                copy.wait_recv()
            total = red1[0]
            for d in range(1, nb):
                total = total + red1[d]
            red2[s] = total
            for d in range(1, ns):
                reduce2.append(
                    send(red2.at[s], red2.at[s], r2s_sem.at[d - 1], r2r_sem.at[d - 1], (b, sector(d)))
                )

    bwd = []
    for n in range(feat // nbk):
        rows = slice(n * nbk, (n + 1) * nbk)
        part = nt(hidden[...], win[rows, :]).reshape(lat_n, lon_n, nbk)
        gmix[:, :, rows] = part
        for side, rim in enumerate(
            (gmix[last_i, :, rows], gmix[0, :, rows], gmix[:, last_j, rows], gmix[:, 0, rows])
        ):
            bedge_s[n, side] = rim.astype(BF16)
        for side, (ci, cj) in enumerate(rim_at):
            bcorn_s[n, side] = gmix[ci, cj : cj + 1, rows]
        sent = []
        for side in range(4):
            sent.append(
                send(
                    bedge_s.at[n, side], bedge_r.at[n, side],
                    bs_sem.at[n, side], br_sem.at[n, side], edge_to[side],
                )
            )
        for side in range(4):
            sent.append(
                send(
                    bcorn_s.at[n, side], bcorn_r.at[n, side],
                    bs_sem.at[n, 4 + side], br_sem.at[n, 4 + side], corner_to[side],
                )
            )
        bwd.append(sent)

    def preunmix(k, carry):
        cols = pl.ds(pl.multiple_of(k * cw, cw), cw)
        taps = [coef[8 - t : 9 - t, cols] for t in range(9)]
        for i, summed in enumerate(inner_rows(lambda r: gmix[r, :, cols], taps, lat_n, lon_n)):
            acc[0, i, :, cols] = direc[i, :, cols] + obs[i * lon_n : (i + 1) * lon_n, cols] + summed
        return carry

    lax.fori_loop(0, feat // cw, preunmix, 0)

    for copy in reduce2:
        copy.wait_recv()
    total = red2[0]
    for d in range(1, ns):
        total = total + red2[d]
    total = jnp.sum(total, axis=1, keepdims=True)
    alpha = total[0:1] / total[1:2]

    for n in range(feat // nbk):
        for copy in bwd[n]:
            copy.wait_recv()

        def unmix(k, carry):
            cols = pl.ds(pl.multiple_of(n * nbk + k * cw, cw), cw)
            inner = pl.ds(pl.multiple_of(k * cw, cw), cw)
            taps = [coef[8 - t : 9 - t, cols] for t in range(9)]
            for i, rim in enumerate(rims_in(bedge_r.at[n], bcorn_r.at[n], taps, inner)):
                out_ref[i, :, cols] = res[i, :, cols] - alpha * (acc[0, i, :, cols] + rim)
            return carry

        lax.fori_loop(0, nbk // cw, unmix, 0)

    for sent in fwd + [phase1, phase2, reduce1, reduce2] + bwd:
        for copy in sent:
            copy.wait_send()


def shards(
    nb, ns,
    base_state, direction, residual, mix_coef, w_in, w_out,
    obs_patch, obs_count, obs_pos, obs_wgt, obs_rinv,
):
    lat_n, lon_n, feat = base_state.shape
    hid = w_in.shape[1]
    slot_n, tap_n = obs_pos.shape[2:]
    tok_n = lat_n * lon_n
    block_n = nb * ns
    n1 = min(512, hid)
    n2 = min(512, feat)
    nbk = min(512, feat)
    patch = obs_patch[0].T
    count = obs_count
    pos = jnp.transpose(obs_pos[0], (1, 2, 0)).reshape(slot_n * tap_n, block_n)
    wgt = jnp.transpose(obs_wgt[0], (1, 2, 0)).reshape(slot_n * tap_n, block_n)
    rinv = obs_rinv[0].T
    stations = slot_n * block_n
    dma = pltpu.SemaphoreType.DMA
    vmem = pltpu.VMEM
    chunks = feat // nbk
    cw = min(256, nbk)
    scratch = [
        vmem((lat_n, lon_n, feat), F32), vmem((lat_n, lon_n, feat), F32), vmem((lat_n, lon_n, feat), F32),
        vmem(mix_coef.shape, F32), vmem(w_in.shape, BF16), vmem(w_out.shape, BF16),
        vmem(patch.shape, jnp.int32), vmem(count.shape, jnp.int32), vmem(pos.shape, jnp.int32),
        vmem(wgt.shape, F32), vmem(rinv.shape, F32),
        vmem((2, lat_n, lon_n, feat), F32), vmem((2 * tok_n, feat), BF16), vmem((tok_n, hid), F32),
        vmem((tok_n, hid), BF16), vmem((tok_n, feat), BF16), vmem((stations, feat), F32),
        vmem((stations, tok_n), BF16), vmem((tok_n, feat), F32), vmem((tok_n, feat), BF16),
        vmem((lat_n, lon_n, feat), F32),
        vmem((2, 4, 16, feat), BF16), vmem((2, 4, 16, feat), BF16),
        vmem((2, 4, 1, feat), F32), vmem((2, 4, 1, feat), F32),
        vmem((chunks, 4, 16, nbk), BF16), vmem((chunks, 4, 16, nbk), BF16),
        vmem((chunks, 4, 1, nbk), F32), vmem((chunks, 4, 1, nbk), F32),
        vmem((LANES, block_n), F32), vmem((nb, ns, LANES), F32), vmem((nb, ns, LANES), F32),
        vmem((ns, nb, LANES), F32), vmem((ns, nb, LANES), F32),
        vmem((2, LANES), F32), vmem((nb, 2, LANES), F32), vmem((ns, 2, LANES), F32),
        dma((11,)), dma((2, 8)), dma((2, 8)), dma((chunks, 8)), dma((chunks, 8)),
        dma((nb - 1,)), dma((nb - 1,)), dma((ns - 1,)), dma((ns - 1,)),
        dma((nb - 1,)), dma((nb - 1,)), dma((ns - 1,)), dma((ns - 1,)),
    ]
    sizes = (nb, ns, lat_n, lon_n, feat, hid, slot_n, tap_n, n1, n2, nbk, cw)
    return pl.pallas_call(
        functools.partial(kernel, sizes),
        out_shape=pltpu.VMEM(base_state.shape, F32),
        in_specs=[pl.BlockSpec(memory_space=pl.ANY)] * 11,
        out_specs=pl.BlockSpec(memory_space=pltpu.VMEM),
        scratch_shapes=scratch,
        compiler_params=pltpu.CompilerParams(
            collective_id=0, has_side_effects=True, vmem_limit_bytes=56 * 2**20
        ),
    )(base_state, direction, residual, mix_coef, w_in, w_out, patch, count, pos, wgt, rinv)


def solution(mesh):
    return jax.shard_map(
        functools.partial(shards, mesh.shape["band"], mesh.shape["sector"]),
        mesh=mesh,
        in_specs=(
            P("band", "sector", None),
            P("band", "sector", None),
            P("band", "sector", None),
            P(),
            P(),
            P(),
            P(("band", "sector"), None, None),
            P(("band", "sector"), None),
            P(("band", "sector"), None, None, None),
            P(("band", "sector"), None, None, None),
            P(("band", "sector"), None, None),
        ),
        out_specs=P("band", "sector", None),
        check_vma=False,
    )
```

time: 51.4 us -> 41.9 us (0.82)
  Pallas kernels: 48.6 us -> 40.6 us
  local copies, waits for them, and re-layouts: 2.69 us -> 1.15 us
    pallas_call x1, Pallas kernels: 48.6 us -> 40.6 us  [shards(): pl.pallas_call(functools.partial(kernel, sizes), out_shape=pltpu.VMEM(bas...]
    unnamed x1, local copies, waits for them, and re-layouts: 2.69 us -> 1.15 us
where the time goes in v2:
time: 41.9 us; the launch traced here: 41.8 us
  Pallas kernels  40.6 us (97%)
  local copies, waits for them, and re-layouts  1.15 us (3%)
    pallas_call x1, Pallas kernels, shards(): pl.pallas_call(functools.partial(kernel, sizes), out_shape=pltpu.VMEM(bas...  40.6 us
    unnamed x1, local copies, waits for them, and re-layouts  1.15 us

profile of v2, /device:TPU:1, one launch (start us, length us, event | category | flops | bytes accessed | tf_op | source)
XLA Modules:
  0.0 41.8 jit_solution(6873063395977411234)
XLA Ops:
  0.0 40.6 %shard_map.109 = f32[16,16,1536]{2,1,0:T(8,128)S(1)} custom-call(f32[16,16,1536]{2,1,0:T(8,128)} %base_h.1, f32[16,16,1536]{2,1,0:T(8,128)} %dir_h.1, f32[16,16,1536]{2,1,0:T(8,128)} %res_h.1, f32[9,1536]{1,0:T(8,128)} %coef_h.1, bf16[1536,3072]{1,0:T(8,128)(2,1)} %win_h.1, bf16[3072,1536]{1,0:T(8,128)(2,1)} %wout_h.1, s32[4,128]{1,0:T(4,128)} %bitcast.18, ...), custom_call_target="tpu_custom_call" | custom-call | tf_op jit(solution)/shard_map/pallas_call | solution.py:442
  40.6 1.1 %copy.13 = f32[16,16,1536]{2,1,0:T(8,128)} copy(f32[16,16,1536]{2,1,0:T(8,128)S(1)} %shard_map.109) | data formatting | bytes 3145728

commit v3 on v2

--- a/solution.py
+++ b/solution.py
@@ -62,10 +62,8 @@
         before, now = now, after
 
 
-def rim_rows(north, south, west, east, corners, coef, lat_n, lon_n):
-    width = west.shape[1]
-    lat_at = lax.broadcasted_iota(jnp.int32, (lat_n, width), 0)
-    lon_at = lax.broadcasted_iota(jnp.int32, (lon_n, width), 0)
+def rim_shares(north, south, west, east, corners, coef, lat_n, lon_n):
+    lat_at = lax.broadcasted_iota(jnp.int32, (lat_n, west.shape[1]), 0)
 
     def column(mid, above, below, b):
         prev = jnp.where(lat_at == 0, above, pltpu.roll(mid, 1, 0))
@@ -74,13 +72,9 @@
 
     rim_w = column(west, corners[0], corners[2], 0)
     rim_e = column(east, corners[1], corners[3], 2)
-    for i in range(lat_n):
-        rim = jnp.where(lon_at == 0, rim_w[i : i + 1], 0.0) + jnp.where(lon_at == lon_n - 1, rim_e[i : i + 1], 0.0)
-        if i == 0:
-            rim = rim + shifted([coef[b] * north for b in range(3)], lon_n)
-        if i == lat_n - 1:
-            rim = rim + shifted([coef[6 + b] * south for b in range(3)], lon_n)
-        yield rim
+    first = shifted([coef[b] * north for b in range(3)], lon_n)
+    last = shifted([coef[6 + b] * south for b in range(3)], lon_n)
+    return first, last, rim_w, rim_e
 
 
 def kernel(
@@ -88,14 +82,14 @@
     base_h, dir_h, res_h, coef_h, win_h, wout_h, patch_h, count_h, pos_h, wgt_h, rinv_h,
     out_ref,
     base, direc, res, coef, win, wout, patch, count, pos, wgt, rinv,
-    acc, mixed, slopes, hidden, tang, weights, onehot, obs, obs_b, gmix,
+    acc, mixed, rimmed, slopes, hidden, tang, weights, onehot, obs, obs_b, gmix,
     fedge_s, fedge_r, fcorn_s, fcorn_r, bedge_s, bedge_r, bcorn_s, bcorn_r,
     pay, a0, a1, a2, a3, red0, red1, red2,
-    load_sem, fs_sem, fr_sem, bs_sem, br_sem,
-    p1s_sem, p1r_sem, p2s_sem, p2r_sem, r1s_sem, r1r_sem, r2s_sem, r2r_sem,
+    load_sem, fs_sem, fr_sem, bs_sem, br_sem, ps_sem, pr_sem,
 ):
-    nb, ns, lat_n, lon_n, feat, hid, slot_n, tap_n, n1, n2, nbk, cw = sizes
+    nb, ns, lat_n, lon_n, feat, hid, slot_n, tap_n, n1, n2, nbk, cw, nw = sizes
     tok_n = lat_n * lon_n
+    rim_n = 2 * (lat_n + lon_n)
     block_n = nb * ns
     last_i, last_j = lat_n - 1, lon_n - 1
     b = lax.axis_index("band")
@@ -118,10 +112,13 @@
 
     loads = {}
     pairs = dict(
-        base=(base_h, base), dir=(dir_h, direc),
+        base=(base_h, base), dir=(dir_h, direc), coef=(coef_h, coef),
         patch=(patch_h, patch), count=(count_h, count), pos=(pos_h, pos), wgt=(wgt_h, wgt), rinv=(rinv_h, rinv),
-        coef=(coef_h, coef), win=(win_h, win), res=(res_h, res), wout=(wout_h, wout),
     )
+    for n in range(hid // nw):
+        cols = pl.ds(n * nw, nw)
+        pairs[n] = (win_h.at[:, cols], win.at[:, cols])
+    pairs |= dict(res=(res_h, res), wout=(wout_h, wout))
     for at, (name, (src, dst)) in enumerate(pairs.items()):
         loads[name] = pltpu.make_async_copy(src, dst, load_sem.at[at])
         loads[name].start()
@@ -131,7 +128,9 @@
             src_ref=src, dst_ref=dst, send_sem=send_sem, recv_sem=recv_sem, device_id=to, device_id_type=MESH
         )
         copy.start()
-        return copy
+
+    def landed(buffer, sem):
+        pltpu.make_async_copy(buffer, buffer, sem).wait()
 
     rim_at = ((last_i, last_j), (last_i, 0), (0, last_j), (0, 0))
     for at, (name, field) in enumerate((("base", base), ("dir", direc))):
@@ -141,24 +140,10 @@
         for side, (ci, cj) in enumerate(rim_at):
             fcorn_s[at, side] = field[ci, cj : cj + 1]
     pl.semaphore_wait(barrier, len(partners))
-    fwd = []
     for at in range(2):
-        sent = []
         for side in range(4):
-            sent.append(
-                send(
-                    fedge_s.at[at, side], fedge_r.at[at, side],
-                    fs_sem.at[at, side], fr_sem.at[at, side], edge_to[side],
-                )
-            )
-        for side in range(4):
-            sent.append(
-                send(
-                    fcorn_s.at[at, side], fcorn_r.at[at, side],
-                    fs_sem.at[at, 4 + side], fr_sem.at[at, 4 + side], corner_to[side],
-                )
-            )
-        fwd.append(sent)
+            send(fedge_s.at[at, side], fedge_r.at[at, side], fs_sem.at[0], fr_sem.at[0], edge_to[side])
+            send(fcorn_s.at[at, side], fcorn_r.at[at, side], fs_sem.at[1], fr_sem.at[1], corner_to[side])
 
     for name in ("patch", "count", "pos", "wgt", "rinv"):
         loads[name].wait()
@@ -170,33 +155,25 @@
     pay[2 * slot_n : 2 * slot_n + tap_all] = pos[...].astype(F32)
     pay[2 * slot_n + tap_all : 2 * slot_n + 2 * tap_all] = wgt[...]
     a0[...] = jnp.transpose(pay[...]).reshape(nb, ns, LANES)
+
     a1[b] = a0[b]
-    phase1 = []
     for d in range(1, nb):
-        phase1.append(send(a0.at[band(d)], a1.at[b], p1s_sem.at[d - 1], p1r_sem.at[d - 1], (band(d), s)))
+        send(a0.at[band(d)], a1.at[b], ps_sem.at[0], pr_sem.at[0], (band(d), s))
 
     loads["coef"].wait()
-    for at, field in enumerate((base, direc)):
-        def premix(k, carry, at=at, field=field):
-            cols = pl.ds(pl.multiple_of(k * cw, cw), cw)
-            taps = [coef[t : t + 1, cols] for t in range(9)]
-            for i, summed in enumerate(inner_rows(lambda r: field[r, :, cols], taps, lat_n, lon_n)):
-                acc[at, i, :, cols] = summed
-            return carry
-
-        lax.fori_loop(0, feat // cw, premix, 0)
-
-    loads["res"].wait()
-    zero = jnp.zeros((lon_n, LANES), F32)
-
-    def square(i, carry):
-        norm, grow = carry
-        r, d = res[i], direc[i]
-        return norm + fold_lanes(r * r), grow + fold_lanes(d * d)
-
-    norm, grow = lax.fori_loop(0, lat_n, square, (zero, zero))
-    red0[0:1] = jnp.sum(norm, axis=0, keepdims=True)
-    red0[1:2] = jnp.sum(grow, axis=0, keepdims=True)
+
+    def premix(at, field, cols):
+        taps = [coef[t : t + 1, cols] for t in range(9)]
+        for i, summed in enumerate(inner_rows(lambda r: field[r, :, cols], taps, lat_n, lon_n)):
+            acc[at, i, :, cols] = summed
+            start = at * tok_n + i * lon_n
+            mixed[start : start + lon_n, cols] = summed.astype(BF16)
+
+    def premix_base(k, carry):
+        premix(0, base, pl.ds(pl.multiple_of(k * cw, cw), cw))
+        return carry
+
+    lax.fori_loop(0, feat // cw, premix_base, 0)
 
     inside_n = (b > 0).astype(F32)
     inside_s = (b < nb - 1).astype(F32)
@@ -207,47 +184,82 @@
         south = edge.at[1][:, cols].astype(F32) * inside_s
         west = edge.at[2][:, cols].astype(F32)
         east = edge.at[3][:, cols].astype(F32)
-        return rim_rows(north, south, west, east, corners, taps, lat_n, lon_n)
-
-    def postmix(at, cols):
-        taps = [coef[t : t + 1, cols] for t in range(9)]
-        for i, rim in enumerate(rims_in(fedge_r.at[at], fcorn_r.at[at], taps, cols)):
-            start = at * tok_n + i * lon_n
-            mixed[start : start + lon_n, cols] = (acc[at, i, :, cols] + rim).astype(BF16)
-
-    for copy in fwd[0]:
-        copy.wait_recv()
-
-    def postmix_base(k, carry):
-        postmix(0, pl.ds(pl.multiple_of(k * cw, cw), cw))
-        return carry
-
-    lax.fori_loop(0, feat // cw, postmix_base, 0)
-    loads["win"].wait()
-
-    phase2 = []
-    posts = [slice(k * cw, (k + 1) * cw) for k in range(feat // cw)]
-    half = hid // n1 // 2
-    for n in range(hid // n1):
+        return rim_shares(north, south, west, east, corners, taps, lat_n, lon_n)
+
+    steps = hid // n1
+    parts = feat // cw
+    share = -(-parts // steps)
+    for n in range(steps):
+        if n * n1 % nw == 0:
+            loads[n * n1 // nw].wait()
         cols = slice(n * n1, (n + 1) * n1)
         slopes[:, cols] = gelu_slope(nn(mixed[:tok_n], win[:, cols]))
-        if n == 0:
-            for copy in phase1:
-                copy.wait_recv()
+        for k in range(n * share, min((n + 1) * share, parts)):
+            premix(1, direc, slice(k * cw, (k + 1) * cw))
+    for n in range(steps):
+        cols = slice(n * n1, (n + 1) * n1)
+        hidden[:, cols] = (slopes[:, cols] * nn(mixed[tok_n:], win[:, cols])).astype(BF16)
+        if n == steps // 3:
+            landed(a1.at[pl.ds(0, nb - 1)], pr_sem.at[0])
             for q in range(ns):
                 a2[q] = a1[:, q, :]
             a3[s] = a2[s]
             for d in range(1, ns):
-                phase2.append(
-                    send(a2.at[sector(d)], a3.at[s], p2s_sem.at[d - 1], p2r_sem.at[d - 1], (b, sector(d)))
-                )
-        if n == half - 1:
-            for copy in fwd[1]:
-                copy.wait_recv()
-        if n >= half:
-            share = -(-len(posts) // (hid // n1 - half))
-            for part in posts[(n - half) * share : (n - half + 1) * share]:
-                postmix(1, part)
+                send(a2.at[sector(d)], a3.at[s], ps_sem.at[1], pr_sem.at[1], (b, sector(d)))
+
+    loads["res"].wait()
+    zero = jnp.zeros((lon_n, LANES), F32)
+
+    def square(i, carry):
+        norm, grow = carry
+        r, d = res[i], direc[i]
+        return norm + fold_lanes(r * r), grow + fold_lanes(d * d)
+
+    norm, grow = lax.fori_loop(0, lat_n, square, (zero, zero))
+    red0[0:1] = jnp.sum(norm, axis=0, keepdims=True)
+    red0[1:2] = jnp.sum(grow, axis=0, keepdims=True)
+
+    landed(fedge_r, fr_sem.at[0])
+    landed(fcorn_r, fr_sem.at[1])
+
+    def postmix(k, carry):
+        cols = pl.ds(pl.multiple_of(k * cw, cw), cw)
+        taps = [coef[t : t + 1, cols] for t in range(9)]
+        for at in range(2):
+            first, last, rim_w, rim_e = rims_in(fedge_r.at[at], fcorn_r.at[at], taps, cols)
+            lon_at = lax.broadcasted_iota(jnp.int32, first.shape, 0)
+            rows = []
+            for i, own in ((0, first), (last_i, last)):
+                ends = jnp.where(lon_at == 0, rim_w[i : i + 1], 0.0) + jnp.where(lon_at == last_j, rim_e[i : i + 1], 0.0)
+                rows.append(acc[at, i, :, cols] + own + ends)
+            rows.append(acc[at, :, 0, cols] + rim_w)
+            rows.append(acc[at, :, last_j, cols] + rim_e)
+            start = at * rim_n
+            for row in rows:
+                rimmed[start : start + row.shape[0], cols] = row.astype(BF16)
+                start += row.shape[0]
+        return carry
+
+    lax.fori_loop(0, feat // cw, postmix, 0)
+    lon_at = lax.broadcasted_iota(jnp.int32, (lon_n, n1), 0)
+    for n in range(steps):
+        cols = slice(n * n1, (n + 1) * n1)
+        both = nn(rimmed[...], win[:, cols])
+        slope = gelu_slope(both[:rim_n])
+        value = slope * both[rim_n:]
+        slopes[:lon_n, cols] = slope[:lon_n]
+        slopes[last_i * lon_n :, cols] = slope[lon_n : 2 * lon_n]
+        hidden[:lon_n, cols] = value[:lon_n].astype(BF16)
+        hidden[last_i * lon_n :, cols] = value[lon_n : 2 * lon_n].astype(BF16)
+        at_w, at_e = 2 * lon_n, 2 * lon_n + lat_n
+        for i in range(1, last_i):
+            start = i * lon_n
+            slopes[start : start + 1, cols] = slope[at_w + i : at_w + i + 1]
+            slopes[start + last_j : start + lon_n, cols] = slope[at_e + i : at_e + i + 1]
+            inner = hidden[start : start + lon_n, cols].astype(F32)
+            inner = jnp.where(lon_at == 0, value[at_w + i : at_w + i + 1], inner)
+            inner = jnp.where(lon_at == last_j, value[at_e + i : at_e + i + 1], inner)
+            hidden[start : start + lon_n, cols] = inner.astype(BF16)
 
     stations = slot_n * block_n
     rb = min(32, block_n)
@@ -272,26 +284,20 @@
                 summed = summed + jnp.where(chans[k] == here, wgts[k], 0.0)
             weights[c * block_n + r : c * block_n + r + rb, j * LANES : (j + 1) * LANES] = summed
 
-    steps = hid // n1
-    for n in range(steps):
-        cols = slice(n * n1, (n + 1) * n1)
-        hidden[:, cols] = (slopes[:, cols] * nn(mixed[tok_n:], win[:, cols])).astype(BF16)
-        if n == half:
-            for copy in phase2:
-                copy.wait_recv()
-            loads["wout"].wait()
-        if n > half:
-            share = -(-len(blocks) // (steps - half - 1))
-            for c, r in blocks[(n - half - 1) * share : (n - half) * share]:
-                spread(c, r)
-    for c in range(slot_n):
-        place(c)
-
     seen = jnp.zeros((stations, LANES), F32)
+    loads["wout"].wait()
     for n in range(feat // n2):
         cols = slice(n * n2, (n + 1) * n2)
         own = direc[:, :, cols].reshape(tok_n, n2)
         tang[:, cols] = (own + nn(hidden[...], wout[:, cols])).astype(BF16)
+        if n == max(feat // n2 - 2, 0):
+            landed(a3.at[pl.ds(0, ns - 1)], pr_sem.at[1])
+    for c, r in blocks:
+        spread(c, r)
+    for c in range(slot_n):
+        place(c)
+    for n in range(feat // n2):
+        cols = slice(n * n2, (n + 1) * n2)
         sampled = nn(onehot[...], tang[:, cols])
         seen = seen + fold_lanes(sampled * weights[:, cols])
     misfit = jnp.sum(seen, axis=1, keepdims=True)
@@ -301,10 +307,9 @@
     lane0 = lax.broadcasted_iota(jnp.int32, (1, LANES), 1) == 0
     red0[1:2] = red0[1:2] + jnp.where(lane0, jnp.sum(scaled * misfit, axis=0, keepdims=True), 0.0)
 
-    reduce1 = []
     red1[b] = red0[...]
     for d in range(1, nb):
-        reduce1.append(send(red0, red1.at[b], r1s_sem.at[d - 1], r1r_sem.at[d - 1], (band(d), s)))
+        send(red0, red1.at[b], ps_sem.at[2], pr_sem.at[2], (band(d), s))
 
     for n in range(feat // n2):
         cols = slice(n * n2, (n + 1) * n2)
@@ -315,23 +320,10 @@
         obs[:, cols] = summed
         obs_b[:, cols] = summed.astype(BF16)
 
-    reduce2 = []
     for n in range(hid // n1):
         rows = slice(n * n1, (n + 1) * n1)
         hidden[:, rows] = (slopes[:, rows] * nt(obs_b[...], wout[rows, :])).astype(BF16)
-        if n == half - 1:
-            for copy in reduce1:
-                copy.wait_recv()
-            total = red1[0]
-            for d in range(1, nb):
-                total = total + red1[d]
-            red2[s] = total
-            for d in range(1, ns):
-                reduce2.append(
-                    send(red2.at[s], red2.at[s], r2s_sem.at[d - 1], r2r_sem.at[d - 1], (b, sector(d)))
-                )
-
-    bwd = []
+
     for n in range(feat // nbk):
         rows = slice(n * nbk, (n + 1) * nbk)
         part = nt(hidden[...], win[rows, :]).reshape(lat_n, lon_n, nbk)
@@ -342,22 +334,17 @@
             bedge_s[n, side] = rim.astype(BF16)
         for side, (ci, cj) in enumerate(rim_at):
             bcorn_s[n, side] = gmix[ci, cj : cj + 1, rows]
-        sent = []
         for side in range(4):
-            sent.append(
-                send(
-                    bedge_s.at[n, side], bedge_r.at[n, side],
-                    bs_sem.at[n, side], br_sem.at[n, side], edge_to[side],
-                )
-            )
-        for side in range(4):
-            sent.append(
-                send(
-                    bcorn_s.at[n, side], bcorn_r.at[n, side],
-                    bs_sem.at[n, 4 + side], br_sem.at[n, 4 + side], corner_to[side],
-                )
-            )
-        bwd.append(sent)
+            send(bedge_s.at[n, side], bedge_r.at[n, side], bs_sem.at[0], br_sem.at[0, n], edge_to[side])
+            send(bcorn_s.at[n, side], bcorn_r.at[n, side], bs_sem.at[1], br_sem.at[1, n], corner_to[side])
+        if n == 0:
+            landed(red1.at[pl.ds(0, nb - 1)], pr_sem.at[2])
+            total = red1[0]
+            for d in range(1, nb):
+                total = total + red1[d]
+            red2[s] = total
+            for d in range(1, ns):
+                send(red2.at[s], red2.at[s], ps_sem.at[3], pr_sem.at[3], (b, sector(d)))
 
     def preunmix(k, carry):
         cols = pl.ds(pl.multiple_of(k * cw, cw), cw)
@@ -368,8 +355,7 @@
 
     lax.fori_loop(0, feat // cw, preunmix, 0)
 
-    for copy in reduce2:
-        copy.wait_recv()
+    landed(red2.at[pl.ds(0, ns - 1)], pr_sem.at[3])
     total = red2[0]
     for d in range(1, ns):
         total = total + red2[d]
@@ -377,22 +363,34 @@
     alpha = total[0:1] / total[1:2]
 
     for n in range(feat // nbk):
-        for copy in bwd[n]:
-            copy.wait_recv()
+        landed(bedge_r.at[n], br_sem.at[0, n])
+        landed(bcorn_r.at[n], br_sem.at[1, n])
 
         def unmix(k, carry):
             cols = pl.ds(pl.multiple_of(n * nbk + k * cw, cw), cw)
             inner = pl.ds(pl.multiple_of(k * cw, cw), cw)
             taps = [coef[8 - t : 9 - t, cols] for t in range(9)]
-            for i, rim in enumerate(rims_in(bedge_r.at[n], bcorn_r.at[n], taps, inner)):
+            first, last, rim_w, rim_e = rims_in(bedge_r.at[n], bcorn_r.at[n], taps, inner)
+            lon_at = lax.broadcasted_iota(jnp.int32, first.shape, 0)
+            for i in range(lat_n):
+                rim = jnp.where(lon_at == 0, rim_w[i : i + 1], 0.0) + jnp.where(lon_at == last_j, rim_e[i : i + 1], 0.0)
+                if i == 0:
+                    rim = rim + first
+                if i == last_i:
+                    rim = rim + last
                 out_ref[i, :, cols] = res[i, :, cols] - alpha * (acc[0, i, :, cols] + rim)
             return carry
 
         lax.fori_loop(0, nbk // cw, unmix, 0)
 
-    for sent in fwd + [phase1, phase2, reduce1, reduce2] + bwd:
-        for copy in sent:
-            copy.wait_send()
+    landed(fedge_s, fs_sem.at[0])
+    landed(fcorn_s, fs_sem.at[1])
+    landed(bedge_s, bs_sem.at[0])
+    landed(bcorn_s, bs_sem.at[1])
+    landed(a1.at[pl.ds(0, nb - 1)], ps_sem.at[0])
+    landed(a3.at[pl.ds(0, ns - 1)], ps_sem.at[1])
+    landed(red1.at[pl.ds(0, nb - 1)], ps_sem.at[2])
+    landed(red2.at[pl.ds(0, ns - 1)], ps_sem.at[3])
 
 
 def shards(
@@ -418,12 +416,13 @@
     vmem = pltpu.VMEM
     chunks = feat // nbk
     cw = min(256, nbk)
+    nw = 2 * n1 if hid % (2 * n1) == 0 else n1
     scratch = [
         vmem((lat_n, lon_n, feat), F32), vmem((lat_n, lon_n, feat), F32), vmem((lat_n, lon_n, feat), F32),
         vmem(mix_coef.shape, F32), vmem(w_in.shape, BF16), vmem(w_out.shape, BF16),
         vmem(patch.shape, jnp.int32), vmem(count.shape, jnp.int32), vmem(pos.shape, jnp.int32),
         vmem(wgt.shape, F32), vmem(rinv.shape, F32),
-        vmem((2, lat_n, lon_n, feat), F32), vmem((2 * tok_n, feat), BF16), vmem((tok_n, hid), F32),
+        vmem((2, lat_n, lon_n, feat), F32), vmem((2 * tok_n, feat), BF16), vmem((4 * (lat_n + lon_n), feat), BF16), vmem((tok_n, hid), F32),
         vmem((tok_n, hid), BF16), vmem((tok_n, feat), BF16), vmem((stations, feat), F32),
         vmem((stations, tok_n), BF16), vmem((tok_n, feat), F32), vmem((tok_n, feat), BF16),
         vmem((lat_n, lon_n, feat), F32),
@@ -434,11 +433,9 @@
         vmem((LANES, block_n), F32), vmem((nb, ns, LANES), F32), vmem((nb, ns, LANES), F32),
         vmem((ns, nb, LANES), F32), vmem((ns, nb, LANES), F32),
         vmem((2, LANES), F32), vmem((nb, 2, LANES), F32), vmem((ns, 2, LANES), F32),
-        dma((11,)), dma((2, 8)), dma((2, 8)), dma((chunks, 8)), dma((chunks, 8)),
-        dma((nb - 1,)), dma((nb - 1,)), dma((ns - 1,)), dma((ns - 1,)),
-        dma((nb - 1,)), dma((nb - 1,)), dma((ns - 1,)), dma((ns - 1,)),
+        dma((10 + hid // nw,)), dma((2,)), dma((2,)), dma((2,)), dma((2, chunks)), dma((4,)), dma((4,)),
     ]
-    sizes = (nb, ns, lat_n, lon_n, feat, hid, slot_n, tap_n, n1, n2, nbk, cw)
+    sizes = (nb, ns, lat_n, lon_n, feat, hid, slot_n, tap_n, n1, n2, nbk, cw, nw)
     return pl.pallas_call(
         functools.partial(kernel, sizes),
         out_shape=pltpu.VMEM(base_state.shape, F32),

time: 41.9 us -> 37.3 us (0.89)
  Pallas kernels: 40.6 us -> 36 us
    pallas_call x1, Pallas kernels: 40.6 us -> 36 us  [shards(): pl.pallas_call(functools.partial(kernel, sizes), out_shape=pltpu.VMEM(bas...]
where the time goes in v3:
time: 37.3 us; the launch traced here: 37.2 us
  Pallas kernels  36 us (97%)
  local copies, waits for them, and re-layouts  1.15 us (3%)
    pallas_call x1, Pallas kernels, shards(): pl.pallas_call(functools.partial(kernel, sizes), out_shape=pltpu.VMEM(bas...  36 us
    unnamed x1, local copies, waits for them, and re-layouts  1.15 us

profile of v3, /device:TPU:1, one launch (start us, length us, event | category | flops | bytes accessed | tf_op | source)
XLA Modules:
  0.0 37.2 jit_solution(11907838092750708656)
XLA Ops:
  0.0 36.0 %shard_map.109 = f32[16,16,1536]{2,1,0:T(8,128)S(1)} custom-call(f32[16,16,1536]{2,1,0:T(8,128)} %base_h.1, f32[16,16,1536]{2,1,0:T(8,128)} %dir_h.1, f32[16,16,1536]{2,1,0:T(8,128)} %res_h.1, f32[9,1536]{1,0:T(8,128)} %coef_h.1, bf16[1536,3072]{1,0:T(8,128)(2,1)} %win_h.1, bf16[3072,1536]{1,0:T(8,128)(2,1)} %wout_h.1, s32[4,128]{1,0:T(4,128)} %bitcast.18, ...), custom_call_target="tpu_custom_call" | custom-call | tf_op jit(solution)/shard_map/pallas_call | solution.py:439
  36.0 1.1 %copy.13 = f32[16,16,1536]{2,1,0:T(8,128)} copy(f32[16,16,1536]{2,1,0:T(8,128)S(1)} %shard_map.109) | data formatting | bytes 3145728

commit v4 on v3

--- a/solution.py
+++ b/solution.py
@@ -101,6 +101,23 @@
     def sector(step):
         return lax.rem(s + step + ns, ns)
 
+    loads = {}
+    pairs = dict(
+        coef=(coef_h, coef), base=(base_h, base), dir=(dir_h, direc),
+        patch=(patch_h, patch), count=(count_h, count), pos=(pos_h, pos), wgt=(wgt_h, wgt), rinv=(rinv_h, rinv),
+    )
+    for n in range(hid // nw):
+        cols = pl.ds(n * nw, nw)
+        pairs[n] = (win_h.at[:, cols], win.at[:, cols])
+    later = dict(res=(res_h, res), wout=(wout_h, wout))
+
+    def load(named):
+        for name, (src, dst) in named.items():
+            loads[name] = pltpu.make_async_copy(src, dst, load_sem.at[len(loads)])
+            loads[name].start()
+
+    load(pairs)
+
     edge_to = [(band(1), s), (band(-1), s), (b, sector(1)), (b, sector(-1))]
     corner_to = [
         (band(1), sector(1)), (band(1), sector(-1)), (band(-1), sector(1)), (band(-1), sector(-1)),
@@ -109,19 +126,7 @@
     barrier = pltpu.get_barrier_semaphore()
     for partner in partners:
         pl.semaphore_signal(barrier, inc=1, device_id=partner, device_id_type=MESH)
-
-    loads = {}
-    pairs = dict(
-        base=(base_h, base), dir=(dir_h, direc), coef=(coef_h, coef),
-        patch=(patch_h, patch), count=(count_h, count), pos=(pos_h, pos), wgt=(wgt_h, wgt), rinv=(rinv_h, rinv),
-    )
-    for n in range(hid // nw):
-        cols = pl.ds(n * nw, nw)
-        pairs[n] = (win_h.at[:, cols], win.at[:, cols])
-    pairs |= dict(res=(res_h, res), wout=(wout_h, wout))
-    for at, (name, (src, dst)) in enumerate(pairs.items()):
-        loads[name] = pltpu.make_async_copy(src, dst, load_sem.at[at])
-        loads[name].start()
+    load(later)
 
     def send(src, dst, send_sem, recv_sem, to):
         copy = pltpu.make_async_remote_copy(
@@ -132,18 +137,34 @@
     def landed(buffer, sem):
         pltpu.make_async_copy(buffer, buffer, sem).wait()
 
+    loads["coef"].wait()
+    loads["base"].wait()
+
+    def premix(at, field, cols):
+        taps = [coef[t : t + 1, cols] for t in range(9)]
+        for i, summed in enumerate(inner_rows(lambda r: field[r, :, cols], taps, lat_n, lon_n)):
+            start = at * tok_n + i * lon_n
+            mixed[start : start + lon_n, cols] = summed.astype(BF16)
+            acc[at, i, :, cols] = summed
+
+    def premix_base(k, carry):
+        premix(0, base, pl.ds(pl.multiple_of(k * cw, cw), cw))
+        return carry
+
+    lax.fori_loop(0, feat // cw, premix_base, 0)
+
+    loads["dir"].wait()
     rim_at = ((last_i, last_j), (last_i, 0), (0, last_j), (0, 0))
-    for at, (name, field) in enumerate((("base", base), ("dir", direc))):
-        loads[name].wait()
+    for at, field in enumerate((base, direc)):
         for side, rim in enumerate((field[last_i], field[0], field[:, last_j], field[:, 0])):
-            fedge_s[at, side] = rim.astype(BF16)
+            fedge_s[side, at] = rim.astype(BF16)
         for side, (ci, cj) in enumerate(rim_at):
-            fcorn_s[at, side] = field[ci, cj : cj + 1]
+            fcorn_s[side, at] = field[ci, cj : cj + 1]
     pl.semaphore_wait(barrier, len(partners))
-    for at in range(2):
-        for side in range(4):
-            send(fedge_s.at[at, side], fedge_r.at[at, side], fs_sem.at[0], fr_sem.at[0], edge_to[side])
-            send(fcorn_s.at[at, side], fcorn_r.at[at, side], fs_sem.at[1], fr_sem.at[1], corner_to[side])
+    for side in range(4):
+        send(fcorn_s.at[side], fcorn_r.at[side], fs_sem.at[1], fr_sem.at[1], corner_to[side])
+    for side in (2, 3, 0, 1):
+        send(fedge_s.at[side], fedge_r.at[side], fs_sem.at[0], fr_sem.at[0], edge_to[side])
 
     for name in ("patch", "count", "pos", "wgt", "rinv"):
         loads[name].wait()
@@ -159,21 +180,6 @@
     a1[b] = a0[b]
     for d in range(1, nb):
         send(a0.at[band(d)], a1.at[b], ps_sem.at[0], pr_sem.at[0], (band(d), s))
-
-    loads["coef"].wait()
-
-    def premix(at, field, cols):
-        taps = [coef[t : t + 1, cols] for t in range(9)]
-        for i, summed in enumerate(inner_rows(lambda r: field[r, :, cols], taps, lat_n, lon_n)):
-            acc[at, i, :, cols] = summed
-            start = at * tok_n + i * lon_n
-            mixed[start : start + lon_n, cols] = summed.astype(BF16)
-
-    def premix_base(k, carry):
-        premix(0, base, pl.ds(pl.multiple_of(k * cw, cw), cw))
-        return carry
-
-    lax.fori_loop(0, feat // cw, premix_base, 0)
 
     inside_n = (b > 0).astype(F32)
     inside_s = (b < nb - 1).astype(F32)
@@ -222,25 +228,21 @@
     landed(fedge_r, fr_sem.at[0])
     landed(fcorn_r, fr_sem.at[1])
 
-    def postmix(k, carry):
-        cols = pl.ds(pl.multiple_of(k * cw, cw), cw)
+    for k in range(feat // nbk):
+        cols = slice(k * nbk, (k + 1) * nbk)
         taps = [coef[t : t + 1, cols] for t in range(9)]
         for at in range(2):
-            first, last, rim_w, rim_e = rims_in(fedge_r.at[at], fcorn_r.at[at], taps, cols)
+            first, last, rim_w, rim_e = rims_in(fedge_r.at[:, at], fcorn_r.at[:, at], taps, cols)
             lon_at = lax.broadcasted_iota(jnp.int32, first.shape, 0)
-            rows = []
-            for i, own in ((0, first), (last_i, last)):
-                ends = jnp.where(lon_at == 0, rim_w[i : i + 1], 0.0) + jnp.where(lon_at == last_j, rim_e[i : i + 1], 0.0)
-                rows.append(acc[at, i, :, cols] + own + ends)
-            rows.append(acc[at, :, 0, cols] + rim_w)
-            rows.append(acc[at, :, last_j, cols] + rim_e)
+            rows = [acc[at, :, 0, cols] + rim_w, acc[at, :, last_j, cols] + rim_e]
+            for i, share in ((0, first), (last_i, last)):
+                row = acc[at, i, :, cols] + share
+                row = jnp.where(lon_at == 0, row + rim_w[i : i + 1], row)
+                rows.insert(-2, jnp.where(lon_at == last_j, row + rim_e[i : i + 1], row))
             start = at * rim_n
             for row in rows:
                 rimmed[start : start + row.shape[0], cols] = row.astype(BF16)
                 start += row.shape[0]
-        return carry
-
-    lax.fori_loop(0, feat // cw, postmix, 0)
     lon_at = lax.broadcasted_iota(jnp.int32, (lon_n, n1), 0)
     for n in range(steps):
         cols = slice(n * n1, (n + 1) * n1)
@@ -313,10 +315,7 @@
 
     for n in range(feat // n2):
         cols = slice(n * n2, (n + 1) * n2)
-        deposit = scaled * weights[:, cols]
-        rough = deposit.astype(BF16)
-        fine = (deposit - rough.astype(F32)).astype(BF16)
-        summed = tn(onehot[...], rough) + tn(onehot[...], fine)
+        summed = tn(onehot[...], (scaled * weights[:, cols]).astype(BF16))
         obs[:, cols] = summed
         obs_b[:, cols] = summed.astype(BF16)
 
@@ -331,13 +330,10 @@
         for side, rim in enumerate(
             (gmix[last_i, :, rows], gmix[0, :, rows], gmix[:, last_j, rows], gmix[:, 0, rows])
         ):
-            bedge_s[n, side] = rim.astype(BF16)
+            bedge_s[side, :, rows] = rim.astype(BF16)
         for side, (ci, cj) in enumerate(rim_at):
-            bcorn_s[n, side] = gmix[ci, cj : cj + 1, rows]
-        for side in range(4):
-            send(bedge_s.at[n, side], bedge_r.at[n, side], bs_sem.at[0], br_sem.at[0, n], edge_to[side])
-            send(bcorn_s.at[n, side], bcorn_r.at[n, side], bs_sem.at[1], br_sem.at[1, n], corner_to[side])
-        if n == 0:
+            bcorn_s[side, :, rows] = gmix[ci, cj : cj + 1, rows]
+        if n == 1:
             landed(red1.at[pl.ds(0, nb - 1)], pr_sem.at[2])
             total = red1[0]
             for d in range(1, nb):
@@ -346,6 +342,11 @@
             for d in range(1, ns):
                 send(red2.at[s], red2.at[s], ps_sem.at[3], pr_sem.at[3], (b, sector(d)))
 
+    for side in range(4):
+        send(bcorn_s.at[side], bcorn_r.at[side], bs_sem.at[1], br_sem.at[1], corner_to[side])
+    for side in (2, 3, 0, 1):
+        send(bedge_s.at[side], bedge_r.at[side], bs_sem.at[0], br_sem.at[0], edge_to[side])
+
     def preunmix(k, carry):
         cols = pl.ds(pl.multiple_of(k * cw, cw), cw)
         taps = [coef[8 - t : 9 - t, cols] for t in range(9)]
@@ -362,26 +363,24 @@
     total = jnp.sum(total, axis=1, keepdims=True)
     alpha = total[0:1] / total[1:2]
 
-    for n in range(feat // nbk):
-        landed(bedge_r.at[n], br_sem.at[0, n])
-        landed(bcorn_r.at[n], br_sem.at[1, n])
-
-        def unmix(k, carry):
-            cols = pl.ds(pl.multiple_of(n * nbk + k * cw, cw), cw)
-            inner = pl.ds(pl.multiple_of(k * cw, cw), cw)
-            taps = [coef[8 - t : 9 - t, cols] for t in range(9)]
-            first, last, rim_w, rim_e = rims_in(bedge_r.at[n], bcorn_r.at[n], taps, inner)
-            lon_at = lax.broadcasted_iota(jnp.int32, first.shape, 0)
-            for i in range(lat_n):
-                rim = jnp.where(lon_at == 0, rim_w[i : i + 1], 0.0) + jnp.where(lon_at == last_j, rim_e[i : i + 1], 0.0)
-                if i == 0:
-                    rim = rim + first
-                if i == last_i:
-                    rim = rim + last
-                out_ref[i, :, cols] = res[i, :, cols] - alpha * (acc[0, i, :, cols] + rim)
-            return carry
-
-        lax.fori_loop(0, nbk // cw, unmix, 0)
+    landed(bedge_r, br_sem.at[0])
+    landed(bcorn_r, br_sem.at[1])
+
+    def unmix(k, carry):
+        cols = pl.ds(pl.multiple_of(k * cw, cw), cw)
+        taps = [coef[8 - t : 9 - t, cols] for t in range(9)]
+        first, last, rim_w, rim_e = rims_in(bedge_r, bcorn_r, taps, cols)
+        lon_at = lax.broadcasted_iota(jnp.int32, first.shape, 0)
+        for i in range(lat_n):
+            rim = jnp.where(lon_at == 0, rim_w[i : i + 1], 0.0) + jnp.where(lon_at == last_j, rim_e[i : i + 1], 0.0)
+            if i == 0:
+                rim = rim + first
+            if i == last_i:
+                rim = rim + last
+            out_ref[i, :, cols] = res[i, :, cols] - alpha * (acc[0, i, :, cols] + rim)
+        return carry
+
+    lax.fori_loop(0, feat // cw, unmix, 0)
 
     landed(fedge_s, fs_sem.at[0])
     landed(fcorn_s, fs_sem.at[1])
@@ -414,7 +413,6 @@
     stations = slot_n * block_n
     dma = pltpu.SemaphoreType.DMA
     vmem = pltpu.VMEM
-    chunks = feat // nbk
     cw = min(256, nbk)
     nw = 2 * n1 if hid % (2 * n1) == 0 else n1
     scratch = [
@@ -426,14 +424,14 @@
         vmem((tok_n, hid), BF16), vmem((tok_n, feat), BF16), vmem((stations, feat), F32),
         vmem((stations, tok_n), BF16), vmem((tok_n, feat), F32), vmem((tok_n, feat), BF16),
         vmem((lat_n, lon_n, feat), F32),
-        vmem((2, 4, 16, feat), BF16), vmem((2, 4, 16, feat), BF16),
-        vmem((2, 4, 1, feat), F32), vmem((2, 4, 1, feat), F32),
-        vmem((chunks, 4, 16, nbk), BF16), vmem((chunks, 4, 16, nbk), BF16),
-        vmem((chunks, 4, 1, nbk), F32), vmem((chunks, 4, 1, nbk), F32),
+        vmem((4, 2, 16, feat), BF16), vmem((4, 2, 16, feat), BF16),
+        vmem((4, 2, 1, feat), F32), vmem((4, 2, 1, feat), F32),
+        vmem((4, 16, feat), BF16), vmem((4, 16, feat), BF16),
+        vmem((4, 1, feat), F32), vmem((4, 1, feat), F32),
         vmem((LANES, block_n), F32), vmem((nb, ns, LANES), F32), vmem((nb, ns, LANES), F32),
         vmem((ns, nb, LANES), F32), vmem((ns, nb, LANES), F32),
         vmem((2, LANES), F32), vmem((nb, 2, LANES), F32), vmem((ns, 2, LANES), F32),
-        dma((10 + hid // nw,)), dma((2,)), dma((2,)), dma((2,)), dma((2, chunks)), dma((4,)), dma((4,)),
+        dma((10 + hid // nw,)), dma((2,)), dma((2,)), dma((2,)), dma((2,)), dma((4,)), dma((4,)),
     ]
     sizes = (nb, ns, lat_n, lon_n, feat, hid, slot_n, tap_n, n1, n2, nbk, cw, nw)
     return pl.pallas_call(

time: 37.3 us -> 36.1 us (0.968); the launches traced: 37.2 us -> 35.6 us
  Pallas kernels: 36 us -> 34.5 us
    pallas_call x1, Pallas kernels: 36 us -> 34.5 us  [shards(): pl.pallas_call(functools.partial(kernel, sizes), out_shape=pltpu.VMEM(bas...]
where the time goes in v4:
time: 36.1 us; the launch traced here: 35.6 us
  Pallas kernels  34.5 us (96%)
  local copies, waits for them, and re-layouts  1.15 us (3%)
    pallas_call x1, Pallas kernels, shards(): pl.pallas_call(functools.partial(kernel, sizes), out_shape=pltpu.VMEM(bas...  34.5 us
    unnamed x1, local copies, waits for them, and re-layouts  1.15 us

profile of v4, /device:TPU:1, one launch (start us, length us, event | category | flops | bytes accessed | tf_op | source)
XLA Modules:
  0.0 35.6 jit_solution(16870644500469344833)
XLA Ops:
  0.0 34.5 %shard_map.109 = f32[16,16,1536]{2,1,0:T(8,128)S(1)} custom-call(f32[16,16,1536]{2,1,0:T(8,128)} %base_h.1, f32[16,16,1536]{2,1,0:T(8,128)} %dir_h.1, f32[16,16,1536]{2,1,0:T(8,128)} %res_h.1, f32[9,1536]{1,0:T(8,128)} %coef_h.1, bf16[1536,3072]{1,0:T(8,128)(2,1)} %win_h.1, bf16[3072,1536]{1,0:T(8,128)(2,1)} %wout_h.1, s32[4,128]{1,0:T(4,128)} %bitcast.18, ...), custom_call_target="tpu_custom_call" | custom-call | tf_op jit(solution)/shard_map/pallas_call | solution.py:437
  34.5 1.1 %copy.13 = f32[16,16,1536]{2,1,0:T(8,128)} copy(f32[16,16,1536]{2,1,0:T(8,128)S(1)} %shard_map.109) | data formatting | bytes 3145728

commit v5 on v4

--- a/solution.py
+++ b/solution.py
@@ -333,19 +333,19 @@
             bedge_s[side, :, rows] = rim.astype(BF16)
         for side, (ci, cj) in enumerate(rim_at):
             bcorn_s[side, :, rows] = gmix[ci, cj : cj + 1, rows]
-        if n == 1:
-            landed(red1.at[pl.ds(0, nb - 1)], pr_sem.at[2])
-            total = red1[0]
-            for d in range(1, nb):
-                total = total + red1[d]
-            red2[s] = total
-            for d in range(1, ns):
-                send(red2.at[s], red2.at[s], ps_sem.at[3], pr_sem.at[3], (b, sector(d)))
 
     for side in range(4):
         send(bcorn_s.at[side], bcorn_r.at[side], bs_sem.at[1], br_sem.at[1], corner_to[side])
     for side in (2, 3, 0, 1):
         send(bedge_s.at[side], bedge_r.at[side], bs_sem.at[0], br_sem.at[0], edge_to[side])
+
+    landed(red1.at[pl.ds(0, nb - 1)], pr_sem.at[2])
+    total = red1[0]
+    for d in range(1, nb):
+        total = total + red1[d]
+    red2[s] = total
+    for d in range(1, ns):
+        send(red2.at[s], red2.at[s], ps_sem.at[3], pr_sem.at[3], (b, sector(d)))
 
     def preunmix(k, carry):
         cols = pl.ds(pl.multiple_of(k * cw, cw), cw)

time: 36.1 us -> 35.8 us (level)
  no operation moved by 1% of the time
where the time goes in v5:
time: 35.8 us; the launch traced here: 35.5 us
  Pallas kernels  34.4 us (96%)
  local copies, waits for them, and re-layouts  1.15 us (3%)
    pallas_call x1, Pallas kernels, shards(): pl.pallas_call(functools.partial(kernel, sizes), out_shape=pltpu.VMEM(bas...  34.4 us
    unnamed x1, local copies, waits for them, and re-layouts  1.15 us

profile of v5, /device:TPU:1, one launch (start us, length us, event | category | flops | bytes accessed | tf_op | source)
XLA Modules:
  0.0 35.5 jit_solution(14460408750328586369)
XLA Ops:
  0.0 34.4 %shard_map.109 = f32[16,16,1536]{2,1,0:T(8,128)S(1)} custom-call(f32[16,16,1536]{2,1,0:T(8,128)} %base_h.1, f32[16,16,1536]{2,1,0:T(8,128)} %dir_h.1, f32[16,16,1536]{2,1,0:T(8,128)} %res_h.1, f32[9,1536]{1,0:T(8,128)} %coef_h.1, bf16[1536,3072]{1,0:T(8,128)(2,1)} %win_h.1, bf16[3072,1536]{1,0:T(8,128)(2,1)} %wout_h.1, s32[4,128]{1,0:T(4,128)} %bitcast.18, ...), custom_call_target="tpu_custom_call" | custom-call | tf_op jit(solution)/shard_map/pallas_call | solution.py:437
  34.4 1.1 %copy.13 = f32[16,16,1536]{2,1,0:T(8,128)} copy(f32[16,16,1536]{2,1,0:T(8,128)S(1)} %shard_map.109) | data formatting | bytes 3145728
